TPU v7x, 512 devices: a whole 4x4x16 slice. The times are simulated.
512 devices in a mesh: seq: 32 (over z, core), head: 16 (over x, y).
Axes of the slice: x: 4, y: 4, z: 16, core: 2. Of those that a mesh axis runs over, the one named last changes fastest.
Arguments:
- tokens: bfloat16 [16384, 4096], P('seq', 'head'), may hold values from -8 to 8
- norm_gain: bfloat16 [1, 4096], P(None, 'head'), may hold values from 0.099609375 to 1.8984375
- qkv_weight: bfloat16 [4096, 16, 384], P(None, 'head'), may hold values from -0.109375 to 0.109375
- out_weight: bfloat16 [2048, 4096], P(None, 'head'), may hold values from -0.25 to 0.25
- mem_gate: float32 [16], P('head'), may hold values from -3 to 3
Outputs:
- mixed: bfloat16 [16384, 4096], P('seq', 'head')
All inputs are finite; a program needn't handle non-finite values.
Results may differ from a plain program's by a relative error of at most 0.0074.
Values may be sent and summed in bfloat16 or wider, within the bound.
A program may use at most 64 MiB of HBM per device.

v0:
```python
import jax
import jax.numpy as jnp
from jax import lax
from jax.sharding import PartitionSpec as P

SEG = 2048


EPS = 1e-06


def passed_along(block, axis, distance):
    devices = range(lax.axis_size(axis))
    route = [(i - distance, i) for i in devices if i - distance in devices]
    return lax.ppermute(block, axis, route)


def carried_in(x, axis, combine, identity):
    length, position = (lax.axis_size(axis), lax.axis_index(axis))
    everything = jax.tree.map(lambda part: lax.all_gather(part, axis), x)
    start = jax.tree.map(
        lambda part, zero: jnp.broadcast_to(jnp.asarray(zero, part.dtype), part.shape), x, identity
    )

    def hop(k, before):
        reached = k < position
        new = combine(before, jax.tree.map(lambda part: part[k], everything))
        return jax.tree.map(lambda a, b: jnp.where(reached, a, b), new, before)

    return lax.fori_loop(0, length, hop, start)


def feat(u):
    return jax.nn.elu(u) + 1.0


def add_sum(earlier, later):
    return (earlier[0] + later[0], earlier[1] + later[1])


def on_device(tokens, norm_gain, qkv_weight, out_weight, mem_gate):
    rows = tokens.shape[0]
    width = qkv_weight.shape[0]
    local_heads = qkv_weight.shape[1]
    head_dim = qkv_weight.shape[2] // 3
    weights = qkv_weight.reshape(width, local_heads * 3 * head_dim)
    part_rows = lax.all_gather(tokens, "head", axis=1, tiled=True)
    part_gain = lax.all_gather(norm_gain, "head", axis=1, tiled=True)
    values = part_rows.astype(jnp.float32)
    scaled = (values * part_gain.astype(jnp.float32)).astype(jnp.bfloat16)
    block = weights
    total = jnp.dot(scaled, block, preferred_element_type=jnp.float32)
    total, squares = (total, jnp.sum(values * values, axis=1, keepdims=True))
    rscale = lax.rsqrt(squares / width + EPS)
    raw_all = total * rscale
    span = SEG // rows
    position = lax.axis_index("seq")
    inside = position % span
    scale = 1.0 / jnp.sqrt(jnp.float32(head_dim))
    row_ids = jnp.arange(rows)
    query = raw_all[:, :head_dim].astype(jnp.bfloat16)
    keys = raw_all[:, head_dim : 2 * head_dim].astype(jnp.bfloat16)
    values = raw_all[:, 2 * head_dim :].astype(jnp.bfloat16)
    earlier_k = []
    earlier_v = []
    for back in range(span - 1, 0, -1):
        moved_k, moved_v = passed_along((keys, values), "seq", back)
        earlier_k.append(moved_k)
        earlier_v.append(moved_v)
    window_k = jnp.concatenate(earlier_k, axis=0)
    window_v = jnp.concatenate(earlier_v, axis=0)
    back_of = span - 1 - jnp.arange(window_k.shape[0]) // rows
    window_live = back_of <= inside
    all_k = jnp.concatenate([window_k, keys], axis=0)
    all_v = jnp.concatenate([window_v, values], axis=0)
    own_live = row_ids[:, None] >= row_ids[None, :]
    live = jnp.concatenate(
        [jnp.broadcast_to(window_live[None, :], (rows, window_k.shape[0])), own_live], axis=1
    )
    scores = (
        lax.dot_general(query, all_k, (((1,), (1,)), ((), ())), preferred_element_type=jnp.float32)
        * scale
    )
    scores = jnp.where(live, scores, -1e30)
    top = jnp.max(scores, axis=1, keepdims=True)
    expo = jnp.where(live, jnp.exp(scores - top), 0.0)
    probs = (expo / jnp.sum(expo, axis=1, keepdims=True)).astype(jnp.bfloat16)
    local = jnp.dot(probs, all_v, preferred_element_type=jnp.float32)
    key_feat = feat(keys.astype(jnp.float32))
    term = lax.dot_general(
        key_feat,
        values.astype(jnp.float32),
        (((0,), (0,)), ((), ())),
        precision=lax.Precision.HIGHEST,
    )
    zterm = jnp.sum(key_feat, axis=0, keepdims=True)
    before, zbefore = carried_in(
        (term, zterm), "seq", add_sum, (jnp.zeros_like(term), jnp.zeros_like(zterm))
    )
    window_feat = feat(window_k.astype(jnp.float32)) * window_live[:, None].astype(jnp.float32)
    correction = lax.dot_general(
        window_feat,
        window_v.astype(jnp.float32),
        (((0,), (0,)), ((), ())),
        precision=lax.Precision.HIGHEST,
    )
    memory = before - correction
    norm = zbefore - jnp.sum(window_feat, axis=0, keepdims=True)
    query_feat = feat(query.astype(jnp.float32))
    numer = jnp.dot(query_feat, memory, precision=lax.Precision.HIGHEST)
    denom = jnp.maximum(jnp.sum(query_feat * norm, axis=1, keepdims=True), 1.0)
    retrieved = numer / denom
    gate = jax.nn.sigmoid(mem_gate[0])
    outputs = (gate * retrieved + (1.0 - gate) * local).astype(jnp.bfloat16)
    block = out_weight
    mixed = jnp.dot(
        lax.all_gather(outputs, "head", axis=1, tiled=True),
        block,
        preferred_element_type=jnp.float32,
    )
    return mixed.astype(jnp.bfloat16)


def solution(mesh):
    placed = (P("seq", "head"), P(None, "head"), P(None, "head", None), P(None, "head"), P("head"))
    return jax.shard_map(
        on_device, mesh=mesh, in_specs=placed, out_specs=P("seq", "head"), check_vma=False
    )
```

profile of v0, /device:TPU:1, one launch (start us, length us, event | category | flops | bytes accessed | tf_op | source)
XLA Modules:
  0.0 273.9 jit_solution(9612830536698080959)
XLA Ops:
  6.5 0.7 all-gather.7.cloned.1.call-update
  7.3 0.0 all-gather.11.cloned.1.call-start
  7.3 19.2 %all_gather.19 = bf16[1,4096]{1,0:T(2,128)(2,1)S(1)} all-gather(bf16[1,256]{1,0:T(2,128)(2,1)} %param.8), channel_id=1, replica_groups=mesh['seq'=32,'head'=16] {'head'}, dimensions={1}, use_global_device_ids=true | all-gather | bytes 8704 | tf_op jit(solution)/shard_map/all_gather | solution.py:48
  26.5 61.2 %all-gather.7.cloned.1.call-done = bf16[512,4096]{1,0:T(8,128)(2,1)} async-done(((bf16[512,256]{1,0:T(8,128)(2,1)}), bf16[512,4096]{1,0:T(8,128)(2,1)}) %all-gather.7.cloned.1.call-update) | async-done | bytes 4194320 | tf_op jit(solution)/shard_map/all_gather | solution.py:47
  87.7 3.2 %fusion.1 = f32[512]{0:T(512)S(1)} fusion(bf16[512,4096]{1,0:T(8,128)(2,1)} %all-gather.7.cloned.1.call-done), kind=kLoop, calls=%fused_computation.6 | loop fusion | flops 6290944 | bytes 4196352 | tf_op jit(solution)/shard_map/reduce_sum | solution.py:53
  90.9 0.2 copy-done.3
  91.1 2.3 fusion.13
  93.5 0.7 copy-done.4
  94.2 1.1 fusion.54
  95.3 0.0 all-gather.9.cloned.1.call-start
  96.1 0.1 iota_compare_fusion
  96.2 1.6 fusion.83
  97.9 4.6 %collective-permute-start.2 = (bf16[512,128]{1,0:T(8,128)(2,1)S(1)}, bf16[512,128]{1,0:T(8,128)(2,1)S(1)}, u32[]{:S(2)}, u32[]{:S(2)}) collective-permute-start(bf16[512,128]{1,0:T(8,128)(2,1)S(1)} %get-tuple-element.150), channel_id=1, source_target_pairs={{0,16},{16,32},{32,48},{48,64},{64,80},{80,96},{96,112},{112,128},... | collective-permute-start | bytes 393224 | tf_op jit(solution)/shard_map/ppermute | solution.py:15
  102.5 3.2 %collective-permute-start.1 = (bf16[512,128]{1,0:T(8,128)(2,1)S(1)}, bf16[512,128]{1,0:T(8,128)(2,1)S(1)}, u32[]{:S(2)}, u32[]{:S(2)}) collective-permute-start(bf16[512,128]{1,0:T(8,128)(2,1)S(1)} %get-tuple-element.150), channel_id=1, source_target_pairs={{0,32},{16,48},{32,64},{48,80},{64,96},{80,112},{96,128},{112,144}... | collective-permute-start | bytes 393224 | tf_op jit(solution)/shard_map/ppermute | solution.py:15
  105.7 3.2 %collective-permute-start = (bf16[512,128]{1,0:T(8,128)(2,1)S(1)}, bf16[512,128]{1,0:T(8,128)(2,1)S(1)}, u32[]{:S(2)}, u32[]{:S(2)}) collective-permute-start(bf16[512,128]{1,0:T(8,128)(2,1)S(1)} %get-tuple-element.150), channel_id=1, source_target_pairs={{0,48},{16,64},{32,80},{48,96},{64,112},{80,128},{96,144},{112,160... | collective-permute-start | bytes 393224 | tf_op jit(solution)/shard_map/ppermute | solution.py:15
  108.9 4.7 %collective-permute-start.5 = (bf16[512,128]{1,0:T(8,128)(2,1)}, bf16[512,128]{1,0:T(8,128)(2,1)}, u32[]{:S(2)}, u32[]{:S(2)}) collective-permute-start(bf16[512,128]{1,0:T(8,128)(2,1)} %get-tuple-element.151), channel_id=1, source_target_pairs={{0,16},{16,32},{32,48},{48,64},{64,80},{80,96},{96,112},{112,128},... | collective-permute-start | bytes 393224 | tf_op jit(solution)/shard_map/ppermute | solution.py:15
  113.5 3.8 %collective-permute-start.4 = (bf16[512,128]{1,0:T(8,128)(2,1)}, bf16[512,128]{1,0:T(8,128)(2,1)}, u32[]{:S(2)}, u32[]{:S(2)}) collective-permute-start(bf16[512,128]{1,0:T(8,128)(2,1)} %get-tuple-element.151), channel_id=1, source_target_pairs={{0,32},{16,48},{32,64},{48,80},{64,96},{80,112},{96,128},{112,144}... | collective-permute-start | bytes 393224 | tf_op jit(solution)/shard_map/ppermute | solution.py:15
  117.4 1.0 fusion.53
  118.4 26.9 %all-gather.2 = f32[32,1,128]{2,1,0:T(1,128)S(1)} all-gather(f32[1,1,128]{2,1,0:T(1,128)S(1)} %bitcast.30), channel_id=3, replica_groups=mesh['seq'=32,'head'=16] {'seq'}, dimensions={0}, use_global_device_ids=true | all-gather | bytes 16896 | tf_op jit(solution)/shard_map/all_gather | solution.py:20
  145.3 3.5 %collective-permute-start.3 = (bf16[512,128]{1,0:T(8,128)(2,1)}, bf16[512,128]{1,0:T(8,128)(2,1)}, u32[]{:S(2)}, u32[]{:S(2)}) collective-permute-start(bf16[512,128]{1,0:T(8,128)(2,1)} %get-tuple-element.151), channel_id=1, source_target_pairs={{0,48},{16,64},{32,80},{48,96},{64,112},{80,128},{96,144},{112,160... | collective-permute-start | bytes 393224 | tf_op jit(solution)/shard_map/ppermute | solution.py:15
  148.8 0.4 fusion.25
  149.3 1.8 fusion.84
  151.1 1.9 copy-done.1
  153.0 0.9 fusion.6
  154.0 14.8 %all-gather.11.cloned.1.call-done = f32[4096,128]{1,0:T(8,128)} async-done(((f32[128,128]{1,0:T(8,128)}), f32[4096,128]{1,0:T(8,128)}) %all-gather.11.cloned.1.call-update) | async-done | bytes 2097168 | tf_op jit(solution)/shard_map/all_gather | solution.py:20
  168.7 28.9 %while.16 = (s32[]{:T(128)}, f32[128,128]{1,0:T(8,128)S(1)}, f32[1,128]{1,0:T(1,128)S(1)}, s32[]{:T(128)}, f32[32,128,128]{2,1,0:T(8,128)}, /*index=5*/f32[32,1,128]{2,1,0:T(1,128)S(1)}, s32[]{:T(128)}, s32[]{:T(128)}) while((s32[]{:T(128)}, f32[128,128]{1,0:T(8,128)S(1)}, f32[1,128]{1,0:T(1,128)S(1)}, s32[]{:T(128)}, ...), condition=%wide.region_3.4_spmd.clone, body=%wide.region_2.3_spmd.clone.sunk | while | flops 49540 | bytes 198267 | solution.py:30
  168.7 0.9 add_select_fusion.3
  169.6 0.9 add_select_fusion.3
  170.5 0.9 add_select_fusion.3
  171.4 0.9 add_select_fusion.3
  172.3 0.9 add_select_fusion.3
  173.2 0.9 add_select_fusion.3
  174.1 0.9 add_select_fusion.3
  175.0 0.9 add_select_fusion.3
  176.0 0.9 add_select_fusion.3
  176.9 0.9 add_select_fusion.3
  177.8 0.9 add_select_fusion.3
  178.7 0.9 add_select_fusion.3
  179.6 0.9 add_select_fusion.3
  180.5 0.9 add_select_fusion.3
  181.4 0.9 add_select_fusion.3
  182.3 0.9 add_select_fusion.3
  183.2 0.9 add_select_fusion.3
  184.1 0.9 add_select_fusion.3
  185.0 0.9 add_select_fusion.3
  185.9 0.9 add_select_fusion.3
  186.8 0.9 add_select_fusion.3
  187.7 0.9 add_select_fusion.3
  188.6 0.9 add_select_fusion.3
  189.5 0.9 add_select_fusion.3
  190.4 0.9 add_select_fusion.3
  191.3 0.9 add_select_fusion.3
  192.2 0.9 add_select_fusion.3
  193.1 0.9 add_select_fusion.3
  194.0 0.9 add_select_fusion.3
  195.0 0.9 add_select_fusion.3
  195.9 0.9 add_select_fusion.3
  196.8 0.9 add_select_fusion.3
  197.7 1.3 multiply_reduce_fusion
  199.0 2.3 convolution_subtract_fusion
  201.2 1.3 fusion.18
  202.6 2.9 %fusion.21 = bf16[512,128]{1,0:T(8,128)(2,1)} fusion(f32[512,128]{1,0:T(8,128)S(1)} %fusion.18, f32[512,2048]{1,0:T(8,128)S(1)} %copy-done.2, pred[512,512]{1,0:T(32,128)(4,1)S(1)} %iota_compare_fusion, f32[512]{0:T(512)S(1)} %fusion.6, f32[512]{0:T(512)S(1)} %get-tuple-element.152, pred[2048]{0:T(1024)(128)(4,1)S(1)} %pad.8.clone, ...), kind=kOutput, calls=%fused_computation.25 | convolution fusion | flops 275972096 | bytes 5380100 | tf_op jit(solution)/shard_map/dot_general | solution.py:88
  205.5 58.6 %all-gather.9.cloned.1.call-done = bf16[512,2048]{1,0:T(8,128)(2,1)} async-done(((bf16[512,128]{1,0:T(8,128)(2,1)}), bf16[512,2048]{1,0:T(8,128)(2,1)}) %all-gather.9.cloned.1.call-update) | async-done | bytes 2097168 | tf_op jit(solution)/shard_map/all_gather | solution.py:117
  264.1 3.3 %convolution_convert_fusion = bf16[512,256]{1,0:T(8,128)(2,1)} fusion(bf16[512,2048]{1,0:T(8,128)(2,1)} %all-gather.9.cloned.1.call-done, bf16[2048,256]{1,0:T(8,128)(2,1)} %param.10), kind=kOutput, calls=%fused_computation.20 | convolution fusion | flops 537001984 | bytes 3407872 | tf_op jit(solution)/shard_map/dot_general | solution.py:116
  (62 shorter events, 0.6 us)
Async XLA Ops:
  6.5 84.4 %copy-start = (bf16[4096,1,384]{2,0,1:T(8,128)(2,1)S(1)}, bf16[4096,1,384]{2,0,1:T(8,128)(2,1)}, u32[]{:S(2)}) copy-start(bf16[4096,1,384]{2,0,1:T(8,128)(2,1)} %param.9) | copy-start | bytes 9437188
  6.5 81.1 %all-gather.7.cloned.1.call-start = ((), (), s32[]{:S(2)}) async-start(), calls=%async_computation | async-start | bytes 4456448 | tf_op jit(solution)/shard_map/all_gather | solution.py:47
  7.3 161.5 %all-gather.11.cloned.1.call-start = ((), (), s32[]{:S(2)}) async-start(), calls=%async_computation.2 | async-start | bytes 2162688 | tf_op jit(solution)/shard_map/all_gather | solution.py:20
  87.7 3.4 %copy-start.3 = (bf16[512,4096]{1,0:T(8,128)(2,1)S(1)}, bf16[512,4096]{1,0:T(8,128)(2,1)}, u32[]{:S(2)}) copy-start(bf16[512,4096]{1,0:T(8,128)(2,1)} %all-gather.7.cloned.1.call-done) | copy-start | bytes 12582916
  93.5 0.8 copy-start.4
  95.3 168.8 %all-gather.9.cloned.1.call-start = ((), (), s32[]{:S(2)}) async-start(), calls=%async_computation.1 | async-start | bytes 2228224 | tf_op jit(solution)/shard_map/all_gather | solution.py:117
  97.9 47.4 %collective-permute-start.2 = (bf16[512,128]{1,0:T(8,128)(2,1)S(1)}, bf16[512,128]{1,0:T(8,128)(2,1)S(1)}, u32[]{:S(2)}, u32[]{:S(2)}) collective-permute-start(bf16[512,128]{1,0:T(8,128)(2,1)S(1)} %get-tuple-element.150), channel_id=1, source_target_pairs={{0,16},{16,32},{32,48},{48,64},{64,80},{80,96},{96,112},{112,128},... | collective-permute-start | bytes 393224 | tf_op jit(solution)/shard_map/ppermute | solution.py:15
  102.5 46.4 %collective-permute-start.1 = (bf16[512,128]{1,0:T(8,128)(2,1)S(1)}, bf16[512,128]{1,0:T(8,128)(2,1)S(1)}, u32[]{:S(2)}, u32[]{:S(2)}) collective-permute-start(bf16[512,128]{1,0:T(8,128)(2,1)S(1)} %get-tuple-element.150), channel_id=1, source_target_pairs={{0,32},{16,48},{32,64},{48,80},{64,96},{80,112},{96,128},{112,144}... | collective-permute-start | bytes 393224 | tf_op jit(solution)/shard_map/ppermute | solution.py:15
  105.7 43.2 %collective-permute-start = (bf16[512,128]{1,0:T(8,128)(2,1)S(1)}, bf16[512,128]{1,0:T(8,128)(2,1)S(1)}, u32[]{:S(2)}, u32[]{:S(2)}) collective-permute-start(bf16[512,128]{1,0:T(8,128)(2,1)S(1)} %get-tuple-element.150), channel_id=1, source_target_pairs={{0,48},{16,64},{32,80},{48,96},{64,112},{80,128},{96,144},{112,160... | collective-permute-start | bytes 393224 | tf_op jit(solution)/shard_map/ppermute | solution.py:15
  108.9 90.1 %collective-permute-start.5 = (bf16[512,128]{1,0:T(8,128)(2,1)}, bf16[512,128]{1,0:T(8,128)(2,1)}, u32[]{:S(2)}, u32[]{:S(2)}) collective-permute-start(bf16[512,128]{1,0:T(8,128)(2,1)} %get-tuple-element.151), channel_id=1, source_target_pairs={{0,16},{16,32},{32,48},{48,64},{64,80},{80,96},{96,112},{112,128},... | collective-permute-start | bytes 393224 | tf_op jit(solution)/shard_map/ppermute | solution.py:15
  113.5 85.4 %collective-permute-start.4 = (bf16[512,128]{1,0:T(8,128)(2,1)}, bf16[512,128]{1,0:T(8,128)(2,1)}, u32[]{:S(2)}, u32[]{:S(2)}) collective-permute-start(bf16[512,128]{1,0:T(8,128)(2,1)} %get-tuple-element.151), channel_id=1, source_target_pairs={{0,32},{16,48},{32,64},{48,80},{64,96},{80,112},{96,128},{112,144}... | collective-permute-start | bytes 393224 | tf_op jit(solution)/shard_map/ppermute | solution.py:15
  145.3 4.0 %copy-start.5 = (bf16[512,128]{1,0:T(8,128)(2,1)}, bf16[512,128]{1,0:T(8,128)(2,1)S(1)}, u32[]{:S(2)}) copy-start(bf16[512,128]{1,0:T(8,128)(2,1)S(1)} %collective-permute-done.2) | copy-start | bytes 393220
  145.3 53.7 %collective-permute-start.3 = (bf16[512,128]{1,0:T(8,128)(2,1)}, bf16[512,128]{1,0:T(8,128)(2,1)}, u32[]{:S(2)}, u32[]{:S(2)}) collective-permute-start(bf16[512,128]{1,0:T(8,128)(2,1)} %get-tuple-element.151), channel_id=1, source_target_pairs={{0,48},{16,64},{32,80},{48,96},{64,112},{80,128},{96,144},{112,160... | collective-permute-start | bytes 393224 | tf_op jit(solution)/shard_map/ppermute | solution.py:15
  148.8 2.2 copy-start.6
  148.8 2.3 copy-start.7
  151.1 1.9 copy-start.1
  197.6 4.9 %copy-start.2 = (f32[512,2048]{1,0:T(8,128)S(1)}, f32[512,2048]{1,0:T(8,128)}, u32[]{:S(2)}) copy-start(f32[512,2048]{1,0:T(8,128)} %copy-done.1) | copy-start | bytes 12582916
Sparse Core Ops, SparseCore 0:
  10.3 77.2 all-gather.6
  95.4 73.2 all-gather.10
  205.6 58.4 all-gather.8
where the time goes:
time: 276 us; the launch traced here: 274 us
  waiting for transfers between devices  135 us (49%)
  blocking collectives  46.1 us (17%)
  other arithmetic  35.1 us (13%)
  starting transfers between devices  23.1 us (8%)
  matrix products  14.9 us (5%)
  between operations  14.1 us (5%)
  local copies, waits for them, and re-layouts  4.54 us (2%)
    all_gather x1, waiting for transfers between devices, on_device(): part_rows = lax.all_gather(tokens, 'head', axis=1, tiled=True)  61.2 us
    all_gather x1, waiting for transfers between devices, on_device(): lax.all_gather(outputs, 'head', axis=1, tiled=True)  58.6 us
    select_n x64, other arithmetic, hop(): return jax.tree.map(lambda a, b: jnp.where(reached, a, b), new, before)  28.1 us
    all_gather x1, blocking collectives, carried_in(): everything = jax.tree.map(lambda part: lax.all_gather(part, axis), x)  26.9 us
    ppermute x6, starting transfers between devices, passed_along(): return lax.ppermute(block, axis, route)  23 us
    all_gather x1, blocking collectives, on_device(): part_gain = lax.all_gather(norm_gain, 'head', axis=1, tiled=True)  19.2 us
    all_gather x1, waiting for transfers between devices, carried_in(): everything = jax.tree.map(lambda part: lax.all_gather(part, axis), x)  14.8 us
  transfers between devices with their start and end apart: 9, of which 3 were waited for; matrix products, arithmetic and copies ran while one was open for 13% of the time, Pallas kernels for 0%

commit v1 on v0

v1 whole, which is shorter than its diff:
```python
import functools

import jax
import jax.numpy as jnp
from jax import lax
from jax.experimental import pallas as pl
from jax.experimental.pallas import tpu as pltpu
from jax.sharding import PartitionSpec as P

SEG = 2048
EPS = 1e-06
SIDE = 4
HEADS = SIDE * SIDE
HD = 128
OFFSETS = (0, -1, 1, 2)
MESH = pl.DeviceIdType.MESH
HIGH = lax.Precision.HIGHEST
F32, BF16 = jnp.float32, jnp.bfloat16


def place():
    s, h = lax.axis_index("seq"), lax.axis_index("head")
    return s, h // SIDE, h % SIDE


def around(position, step):
    return lax.rem(position + step + SIDE, SIDE)


def beside(dim, step):
    s, x, y = place()
    if dim == "x":
        return s, around(x, step) * SIDE + y
    return s, x * SIDE + around(y, step)


def greet(partners):
    barrier = pltpu.get_barrier_semaphore()
    for partner in partners:
        pl.semaphore_signal(barrier, inc=1, device_id=partner, device_id_type=MESH)
    pl.semaphore_wait(barrier, len(partners))


def neighbours():
    return [beside(dim, step) for dim in "xy" for step in (1, -1)]


def remote(source, target, sent, landed, partner):
    return pltpu.make_async_remote_copy(
        src_ref=source, dst_ref=target, send_sem=sent, recv_sem=landed,
        device_id=partner, device_id_type=MESH,
    )


class Gather:
    def __init__(self, buf, sent, landed, unit, first_row, rows, dims):
        self.buf, self.sent, self.landed, self.unit = buf, sent, landed, unit
        self.lo, self.rows, self.dims = first_row, rows, dims
        self.started = []

    def slot(self, i, j):
        _, x, y = place()
        along = {self.dims[0]: i, self.dims[1]: j}
        return around(x, along["x"]) * SIDE + around(y, along["y"])

    def view(self, i, j, part):
        half = self.rows // 2
        lo, size = {"all": (0, self.rows), "low": (0, half), "high": (half, half)}[part]
        return self.buf.at[self.slot(i, j), pl.ds(self.lo + lo, size)]

    def copy(self, i, j, part, index, dim, step):
        ref = self.view(i, j, part)
        return remote(ref, ref, self.sent.at[self.unit, index], self.landed.at[self.unit, index], beside(dim, step))

    def send(self, i, j, part, index, dim, step):
        copy = self.copy(i, j, part, index, dim, step)
        copy.start()
        self.started.append(copy)

    def await_first(self, index):
        i, part = ((-1, "all"), (1, "all"), (2, "low"), (2, "high"))[index]
        self.copy(i, 0, part, index, self.dims[0], 1).wait_recv()

    def await_second(self, k, index):
        j, part = ((-1, "all"), (1, "all"), (2, "low"), (2, "high"))[index]
        self.copy(OFFSETS[k], j, part, 4 + 4 * k + index, self.dims[1], 1).wait_recv()

    def out_first(self):
        self.send(0, 0, "all", 0, self.dims[0], 1)
        self.send(0, 0, "all", 1, self.dims[0], -1)

    def out_second(self, k):
        self.send(OFFSETS[k], 0, "all", 4 + 4 * k, self.dims[1], 1)
        self.send(OFFSETS[k], 0, "all", 5 + 4 * k, self.dims[1], -1)

    def on_first(self):
        self.await_first(0)
        self.send(-1, 0, "low", 2, self.dims[0], 1)
        self.out_second(1)
        self.await_first(1)
        self.send(1, 0, "high", 3, self.dims[0], -1)
        self.out_second(2)

    def far_first(self):
        self.await_first(2)
        self.await_first(3)
        self.out_second(3)

    def on_second(self, k):
        self.await_second(k, 0)
        self.send(OFFSETS[k], -1, "low", 6 + 4 * k, self.dims[1], 1)
        self.await_second(k, 1)
        self.send(OFFSETS[k], 1, "high", 7 + 4 * k, self.dims[1], -1)

    def far_second(self, k):
        self.await_second(k, 2)
        self.await_second(k, 3)

    def finish(self):
        for copy in self.started:
            copy.wait_send()


def near_blocks():
    return [(i, j) for i in OFFSETS for j in (0, -1, 1)]


def gather_units(units, multiply):
    pairs = [units[at : at + 2] for at in range(0, len(units), 2)]

    def opening(pair):
        for unit in pair:
            unit.out_first()
        for unit in pair:
            unit.out_second(0)

    def first(pair):
        for unit in pair:
            unit.on_first()

    def second(pair):
        for unit in pair:
            unit.on_second(0)

    def third(pair):
        for unit in pair:
            unit.far_first()

    def fourth(pair):
        for unit in pair:
            unit.on_second(1)
            unit.on_second(2)

    def fifth(pair):
        for unit in pair:
            unit.on_second(3)

    def products(pair):
        for unit in pair:
            multiply(unit, near_blocks(), True)

    def last(pair):
        for unit in pair:
            for k in range(SIDE):
                unit.far_second(k)
            multiply(unit, [(i, 2) for i in OFFSETS], False)

    stages = [opening, first, second, third, fourth, fifth, products, last]
    lag = 2
    for clock in range(len(stages) + lag * (len(pairs) - 1)):
        for at, pair in enumerate(pairs):
            stage = clock - lag * at if clock > 0 else (0 if at < 2 else -1)
            if clock > 0 and at == 1 and stage == 0:
                continue
            if 0 <= stage < len(stages):
                stages[stage](pair)


def make_units(buf, sent, landed, rows, count):
    size = rows // count
    return [
        Gather(buf, sent, landed, u, u * size, size, "yx" if u % 2 == 0 else "xy") for u in range(count)
    ]


def summed_over_plane(own, column, line, sent, landed):
    steps = (1, -1, 2)
    total = own[...]
    copies = []
    for turn, (source, box, dim) in enumerate(((own, column, "y"), (line.at[3], line, "x"))):
        if turn == 1:
            line[3] = total
        turn_copies = []
        for at, step in enumerate(steps):
            index = 3 * turn + at
            copy = remote(source, box.at[at], sent.at[index], landed.at[index], beside(dim, step))
            copy.start()
            turn_copies.append(copy)
        for copy in turn_copies:
            copy.wait_recv()
        for at in range(3):
            total = total + box[at]
        copies += turn_copies
    return total, copies


def qkv_kernel(count, tokens_ref, gain_ref, w_hbm, q_ref, k_ref, v_ref, buf, w_ref, acc, own, column, line,
               sent, landed, small_sent, small_landed, w_sem):
    s, x, y = place()
    w_copy = pltpu.make_async_copy(w_hbm, w_ref, w_sem)
    w_copy.start()
    greet(neighbours() + [beside("x", 2), beside("y", 2)])
    values = tokens_ref[...].astype(F32)
    buf[x * SIDE + y] = (values * gain_ref[...].astype(F32)).astype(BF16)
    rows, width = values.shape
    units = make_units(buf, sent, landed, rows, count)
    waited = []

    def multiply(unit, blocks, first):
        if not waited:
            w_copy.wait()
            waited.append(True)
        at = pl.ds(unit.lo, unit.rows)
        total = None if first else acc[at]
        for i, j in blocks:
            slot = unit.slot(i, j)
            term = jnp.dot(buf[slot, at], w_ref[slot], preferred_element_type=F32)
            total = term if total is None else total + term
        acc[at] = total

    own[...] = lax.dot_general(
        jnp.ones((8, width), F32), values * values, (((1,), (1,)), ((), ())),
        precision=HIGH, preferred_element_type=F32,
    )
    gather_units(units, multiply)
    squares, copies = summed_over_plane(own, column, line, small_sent, small_landed)
    scale = lax.rsqrt(squares / (width * HEADS) + EPS)
    pick = (lax.broadcasted_iota(jnp.int32, (8, HD), 0) == 0).astype(F32)
    spread = lax.dot_general(scale, pick, (((0,), (0,)), ((), ())), precision=HIGH, preferred_element_type=F32)
    q_ref[...] = (acc[:, :HD] * spread).astype(BF16)
    k_ref[...] = (acc[:, HD : 2 * HD] * spread).astype(BF16)
    v_ref[...] = (acc[:, 2 * HD :] * spread).astype(BF16)
    for unit in units:
        unit.finish()
    for copy in copies:
        copy.wait_send()


def project_qkv(tokens, gain, weights):
    rows, width = tokens.shape
    columns = weights.shape[2]
    count = 4
    spec = pl.BlockSpec(memory_space=pltpu.VMEM)
    return pl.pallas_call(
        functools.partial(qkv_kernel, count),
        out_shape=[jax.ShapeDtypeStruct((rows, HD), BF16)] * 3,
        in_specs=[spec, spec, pl.BlockSpec(memory_space=pl.ANY)],
        out_specs=[spec] * 3,
        scratch_shapes=[
            pltpu.VMEM((HEADS, rows, width), BF16),
            pltpu.VMEM((HEADS, width, columns), BF16),
            pltpu.VMEM((rows, columns), F32),
            pltpu.VMEM((8, rows), F32),
            pltpu.VMEM((3, 8, rows), F32),
            pltpu.VMEM((4, 8, rows), F32),
            pltpu.SemaphoreType.DMA((count, 20)),
            pltpu.SemaphoreType.DMA((count, 20)),
            pltpu.SemaphoreType.DMA((6,)),
            pltpu.SemaphoreType.DMA((6,)),
            pltpu.SemaphoreType.DMA,
        ],
        compiler_params=pltpu.CompilerParams(collective_id=0, has_side_effects=True, vmem_limit_bytes=40 << 20),
        name="project_qkv",
    )(tokens, gain, weights)


def out_kernel(count, part_ref, w_hbm, o_ref, buf, w_ref, acc, sent, landed, w_sem):
    s, x, y = place()
    w_copy = pltpu.make_async_copy(w_hbm, w_ref, w_sem)
    w_copy.start()
    greet(neighbours())
    buf[x * SIDE + y] = part_ref[...]
    units = make_units(buf, sent, landed, part_ref.shape[0], count)
    waited = []

    def multiply(unit, blocks, first):
        if not waited:
            w_copy.wait()
            waited.append(True)
        at = pl.ds(unit.lo, unit.rows)
        total = None if first else acc[at]
        for i, j in blocks:
            slot = unit.slot(i, j)
            term = jnp.dot(buf[slot, at], w_ref[slot], preferred_element_type=F32)
            total = term if total is None else total + term
        if first:
            acc[at] = total
        else:
            o_ref[at] = total.astype(BF16)

    gather_units(units, multiply)
    for unit in units:
        unit.finish()


def project_out(part, weights):
    rows = part.shape[0]
    columns = weights.shape[2]
    count = 4
    spec = pl.BlockSpec(memory_space=pltpu.VMEM)
    return pl.pallas_call(
        functools.partial(out_kernel, count),
        out_shape=jax.ShapeDtypeStruct((rows, columns), BF16),
        in_specs=[spec, pl.BlockSpec(memory_space=pl.ANY)],
        out_specs=spec,
        scratch_shapes=[
            pltpu.VMEM((HEADS, rows, HD), BF16),
            pltpu.VMEM((HEADS, HD, columns), BF16),
            pltpu.VMEM((rows, columns), F32),
            pltpu.SemaphoreType.DMA((count, 20)),
            pltpu.SemaphoreType.DMA((count, 20)),
            pltpu.SemaphoreType.DMA,
        ],
        compiler_params=pltpu.CompilerParams(collective_id=1, has_side_effects=True, vmem_limit_bytes=40 << 20),
        name="project_out",
    )(part, weights)


def feat(u):
    return jnp.where(u > 0, u + 1.0, jnp.exp(jnp.minimum(u, 0.0)))


def chip_places():
    s, h = lax.axis_index("seq"), lax.axis_index("head")
    return s, h


SPAN = 4
NORM_ROWS = 16


def attend_kernel(segments, gate_ref, q_ref, k_ref, v_ref, o_ref, kv, o_local, term, parts, seg_term, outgoing, incoming,
                  quarter, memory, kv_sent, kv_landed, a_sent, a_landed, b_sent, b_landed, c_sent, c_landed):
    s, h = chip_places()
    seg, pos = s // SPAN, s % SPAN
    base = seg * SPAN

    def peer(step):
        return base + lax.rem(pos + step, SPAN), h

    mate = (base + lax.rem(pos // 2 * 2 + 1 - pos % 2, SPAN), h)
    across = (base + lax.rem(pos + 2, SPAN), h)
    later = [(lax.rem(s + SPAN * d, segments * SPAN), h) for d in range(1, segments)]
    greet([peer(1), peer(2), peer(3)] + later)

    rows = q_ref.shape[0]
    piece = HD // SPAN
    kv[pos, :, :HD] = k_ref[...]
    kv[pos, :, HD:] = v_ref[...]
    mine = kv.at[pos]
    to_across = remote(mine, mine, kv_sent.at[0], kv_landed.at[0], across)
    to_mate = remote(mine, mine, kv_sent.at[1], kv_landed.at[1], mate)
    to_across.start()
    keys = feat(k_ref[...].astype(F32))
    key_high = keys.astype(BF16)
    term[:HD] = lax.dot_general(key_high, v_ref[...], (((0,), (0,)), ((), ())), preferred_element_type=F32).astype(BF16)
    term[HD:] = jnp.broadcast_to(jnp.sum(keys, axis=0, keepdims=True), (NORM_ROWS, HD)).astype(BF16)
    first = []
    for step in (1, 2, 3):
        to = lax.rem(pos + step, SPAN)
        for at, (lo, size, low) in enumerate(((to * piece, piece, 0), (HD, NORM_ROWS, piece))):
            index = 2 * (step - 1) + at
            copy = remote(term.at[pl.ds(pl.multiple_of(lo, 16), size)], parts.at[step - 1, pl.ds(low, size)],
                          a_sent.at[index], a_landed.at[index], peer(step))
            copy.start()
            first.append(copy)
    to_mate.start()
    for copy in first:
        copy.wait_recv()
    share = jnp.concatenate([term[pl.ds(pl.multiple_of(pos * piece, 16), piece)], term[HD:]], axis=0).astype(F32)
    for at in range(3):
        share = share + parts[at].astype(F32)
    outgoing[...] = share.astype(BF16)

    def second(d):
        return remote(outgoing, incoming.at[d - 1], b_sent.at[d - 1], b_landed.at[d - 1], later[d - 1])

    order = sorted(range(1, segments), key=lambda d: -min(d, segments - d))
    for d in order:
        @pl.when(seg + d < segments)
        def _():
            second(d).start()

    far = lax.rem(pos + 2, SPAN)
    theirs = kv.at[far]
    to_across.wait_recv()
    relay = remote(theirs, theirs, kv_sent.at[2], kv_landed.at[2], mate)
    relay.start()
    to_mate.wait_recv()
    relay.wait_recv()

    factor = float(HD ** -0.5 * 1.4426950408889634)
    chunk = 128
    for r in range(rows // chunk):
        at = pl.ds(r * chunk, chunk)
        query = q_ref[at]
        live_keys = (r + 1) * chunk
        scores = [lax.dot_general(query, kv[pos, :live_keys, :HD], (((1,), (1,)), ((), ())), preferred_element_type=F32)]
        row = lax.broadcasted_iota(jnp.int32, (chunk, live_keys), 0) + r * chunk
        column = lax.broadcasted_iota(jnp.int32, (chunk, live_keys), 1)
        scores[0] = jnp.where(row >= column, scores[0], -1e30)
        tops = [jnp.max(scores[0], axis=1, keepdims=True)]
        biases = [0.0]
        others = []
        for step in (1, 2, 3):
            slot = lax.rem(pos + step, SPAN)
            bias = jnp.where(slot < pos, 0.0, -1e30)
            block = lax.dot_general(query, kv[slot, :, :HD], (((1,), (1,)), ((), ())), preferred_element_type=F32)
            scores.append(block)
            tops.append(jnp.max(block, axis=1, keepdims=True) + bias)
            biases.append(bias)
            others.append(slot)
        top = jnp.maximum(jnp.maximum(tops[0], tops[1]), jnp.maximum(tops[2], tops[3]))
        total = jnp.zeros((chunk, 1), F32)
        mixed = jnp.zeros((chunk, HD), F32)
        for block, bias, value in zip(
            scores, biases, [kv[pos, :live_keys, HD:]] + [kv[slot, :, HD:] for slot in others]
        ):
            expo = jnp.exp2((block - (top - bias)) * factor)
            total = total + jnp.sum(expo, axis=1, keepdims=True)
            mixed = mixed + jnp.dot(expo.astype(BF16), value, preferred_element_type=F32)
        o_local[at] = mixed / total

    share = jnp.zeros((piece + NORM_ROWS, HD), F32)
    quarter[...] = jnp.zeros_like(quarter)
    for d in reversed(order):
        @pl.when(seg - d >= 0)
        def _():
            second(d).wait_recv()
            quarter[...] += incoming[d - 1].astype(F32)
    here = pl.ds(pl.multiple_of(pos * piece, 16), piece)
    memory[here] = quarter[:piece].astype(BF16)
    third = []
    for step in (1, 2, 3):
        copy = remote(memory.at[here], memory.at[here], c_sent.at[step - 1], c_landed.at[step - 1], peer(step))
        copy.start()
        third.append(copy)
    queries = feat(q_ref[...].astype(F32))
    norm = quarter[piece : piece + 1]
    denom = jnp.maximum(jnp.sum(queries * norm, axis=1, keepdims=True), 1.0)
    for step in (1, 2, 3):
        there = pl.ds(pl.multiple_of(lax.rem(pos + SPAN - step, SPAN) * piece, 16), piece)
        remote(memory.at[there], memory.at[there], c_sent.at[step - 1], c_landed.at[step - 1], peer(step)).wait_recv()
    numer = jnp.dot(queries.astype(BF16), memory[...], preferred_element_type=F32)
    gate = jax.nn.sigmoid(jnp.full((1, HD), gate_ref[0], F32))
    o_ref[...] = (gate * (numer / denom) + (1.0 - gate) * o_local[...]).astype(BF16)

    for copy in [to_across, to_mate, relay] + first + third:
        copy.wait_send()
    for d in order:
        @pl.when(seg + d < segments)
        def _():
            second(d).wait_send()


def attend(gate, q, k, v, seq_devices):
    rows = q.shape[0]
    segments = seq_devices // SPAN
    piece = HD // SPAN
    spec = pl.BlockSpec(memory_space=pltpu.VMEM)
    return pl.pallas_call(
        functools.partial(attend_kernel, segments),
        out_shape=jax.ShapeDtypeStruct((rows, HD), BF16),
        in_specs=[pl.BlockSpec(memory_space=pltpu.SMEM), spec, spec, spec],
        out_specs=spec,
        scratch_shapes=[
            pltpu.VMEM((SPAN, rows, 2 * HD), BF16),
            pltpu.VMEM((rows, HD), F32),
            pltpu.VMEM((HD + NORM_ROWS, HD), BF16),
            pltpu.VMEM((3, piece + NORM_ROWS, HD), BF16),
            pltpu.VMEM((piece + NORM_ROWS, HD), F32),
            pltpu.VMEM((piece + NORM_ROWS, HD), BF16),
            pltpu.VMEM((segments - 1, piece + NORM_ROWS, HD), BF16),
            pltpu.VMEM((piece + NORM_ROWS, HD), F32),
            pltpu.VMEM((HD, HD), BF16),
            pltpu.SemaphoreType.DMA((3,)),
            pltpu.SemaphoreType.DMA((3,)),
            pltpu.SemaphoreType.DMA((6,)),
            pltpu.SemaphoreType.DMA((6,)),
            pltpu.SemaphoreType.DMA((segments - 1,)),
            pltpu.SemaphoreType.DMA((segments - 1,)),
            pltpu.SemaphoreType.DMA((3,)),
            pltpu.SemaphoreType.DMA((3,)),
        ],
        compiler_params=pltpu.CompilerParams(collective_id=2, has_side_effects=True, vmem_limit_bytes=40 << 20),
        name="attend",
    )(gate, q, k, v)


def on_device(tokens, norm_gain, qkv_weight, out_weight, mem_gate):
    width = tokens.shape[1]
    weights = qkv_weight.reshape(HEADS, width, 3 * HD)
    q, k, v = project_qkv(tokens, norm_gain, weights)
    part = attend(mem_gate, q, k, v, lax.axis_size("seq"))
    return project_out(part, out_weight.reshape(HEADS, HD, out_weight.shape[1]))


def solution(mesh):
    placed = (P("seq", "head"), P(None, "head"), P(None, "head", None), P(None, "head"), P("head"))
    return jax.shard_map(
        on_device, mesh=mesh, in_specs=placed, out_specs=P("seq", "head"), check_vma=False
    )
```

time: 276 us -> 96.1 us (0.35)
  the two profiles are of different devices: /device:TPU:1 before, /device:TPU:32 now
where the time goes in v1:
time: 96.1 us; the launch traced here: 95.9 us
  Pallas kernels  90.9 us (95%)
  local copies, waits for them, and re-layouts  4.22 us (4%)
    pallas_call x1, Pallas kernels, project_qkv(): pl.pallas_call(functools.partial(qkv_kernel, count), out_shape=[jax.Shape...  41.9 us
    pallas_call x1, Pallas kernels, attend(): pl.pallas_call(functools.partial(attend_kernel, segments), out_shape=jax....  25.9 us
    pallas_call x1, Pallas kernels, project_out(): pl.pallas_call(functools.partial(out_kernel, count), out_shape=jax.ShapeD...  23.1 us
    unnamed x9, local copies, waits for them, and re-layouts  4.22 us

profile of v1, /device:TPU:32, one launch (start us, length us, event | category | flops | bytes accessed | tf_op | source)
XLA Modules:
  0.0 95.9 jit_solution(8189381092190975520)
XLA Ops:
  0.7 0.0 copy-start
  0.7 1.9 %copy-done = bf16[4096,1,384]{2,0,1:T(8,128)(2,1)S(1)} copy-done((bf16[4096,1,384]{2,0,1:T(8,128)(2,1)S(1)}, bf16[4096,1,384]{2,0,1:T(8,128)(2,1)}, u32[]{:S(2)}) %copy-start) | copy-done | bytes 3145752
  2.5 0.0 copy-start.2
  2.5 0.9 copy-done.2
  3.5 0.0 copy-start.3
  3.5 0.7 copy-done.3
  4.2 0.0 copy-start.1
  4.2 41.9 %project_qkv.1 = (bf16[512,128]{1,0:T(8,128)(2,1)S(1)}, bf16[512,128]{1,0:T(8,128)(2,1)S(1)}, bf16[512,128]{1,0:T(8,128)(2,1)S(1)}) custom-call(bf16[512,256]{1,0:T(8,128)(2,1)S(1)} %copy-done.2, bf16[1,256]{1,0:T(2,128)(2,1)S(1)} %copy-done.3, bf16[16,256,384]{2,1,0:T(8,128)(2,1)S(1)} %bitcast.2), custom_call_target="tpu_custom_call" | custom-call | tf_op jit(solution)/shard_map/project_qkv/pallas_call | solution.py:254
  46.1 25.9 %attend.1.part_ref = bf16[512,128]{1,0:T(8,128)(2,1)S(1)} custom-call(f32[1]{0:T(128)S(6)} %copy.7.gate_ref, bf16[512,128]{1,0:T(8,128)(2,1)S(1)} %get-tuple-element.8.q_ref, bf16[512,128]{1,0:T(8,128)(2,1)S(1)} %get-tuple-element.9.k_ref, bf16[512,128]{1,0:T(8,128)(2,1)S(1)} %get-tuple-element.10.v_ref), custom_call_target="tpu_custom_call" | custom-call | tf_op jit(solution)/shard_map/attend/pallas_call | solution.py:471
  72.0 0.0 copy-done.1
  72.0 23.1 %project_out.1 = bf16[512,256]{1,0:T(8,128)(2,1)S(1)} custom-call(bf16[512,128]{1,0:T(8,128)(2,1)S(1)} %attend.1.part_ref, bf16[16,128,256]{2,1,0:T(8,128)(2,1)S(1)} %bitcast.3), custom_call_target="tpu_custom_call" | custom-call | tf_op jit(solution)/shard_map/project_out/pallas_call | solution.py:311
  95.1 0.7 copy.8
Async XLA Ops:
  0.7 1.9 %copy-start = (bf16[4096,1,384]{2,0,1:T(8,128)(2,1)S(1)}, bf16[4096,1,384]{2,0,1:T(8,128)(2,1)}, u32[]{:S(2)}) copy-start(bf16[4096,1,384]{2,0,1:T(8,128)(2,1)} %param.7) | copy-start | bytes 9437188
  2.5 0.9 copy-start.2
  3.5 0.7 copy-start.3
  4.2 67.9 %copy-start.1 = (bf16[2048,256]{1,0:T(8,128)(2,1)S(1)}, bf16[2048,256]{1,0:T(8,128)(2,1)}, u32[]{:S(2)}) copy-start(bf16[2048,256]{1,0:T(8,128)(2,1)} %param.8) | copy-start | bytes 3145732

commit v2 on v0

v2 whole, which is shorter than its diff:
```python
import functools

import jax
import jax.numpy as jnp
from jax import lax
from jax.experimental import pallas as pl
from jax.experimental.pallas import tpu as pltpu
from jax.sharding import PartitionSpec as P

SEG = 2048
EPS = 1e-06
SIDE = 4
HEADS = SIDE * SIDE
HD = 128
OFFSETS = (0, -1, 1, 2)
MESH = pl.DeviceIdType.MESH
HIGH = lax.Precision.HIGHEST
F32, BF16 = jnp.float32, jnp.bfloat16


def place():
    s, h = lax.axis_index("seq"), lax.axis_index("head")
    return s, h // SIDE, h % SIDE


def around(position, step):
    return lax.rem(position + step + SIDE, SIDE)


def remote(source, target, sent, landed, partner):
    return pltpu.make_async_remote_copy(
        src_ref=source, dst_ref=target, send_sem=sent, recv_sem=landed,
        device_id=partner, device_id_type=MESH,
    )


class Plane:
    def __init__(self):
        s, x, y = place()
        xs = {i: around(x, i) for i in OFFSETS}
        ys = {j: around(y, j) for j in OFFSETS}
        self.slots = {(i, j): xs[i] * SIDE + ys[j] for i in OFFSETS for j in OFFSETS}
        self.devices = {("x", i): (s, self.slots[i, 0]) for i in OFFSETS}
        self.devices.update({("y", j): (s, self.slots[0, j]) for j in OFFSETS})

    def neighbours(self):
        return [self.devices[dim, step] for dim in "xy" for step in (1, -1)]


class Gather:
    def __init__(self, plane, buf, sent, landed, unit, first_row, rows, dims, opposite):
        self.plane, self.buf, self.sent, self.landed, self.unit = plane, buf, sent, landed, unit
        self.at, self.dims, self.opposite = pl.ds(first_row, rows), dims, opposite
        self.started = []

    def slot(self, i, j):
        return self.plane.slots[(i, j) if self.dims == "xy" else (j, i)]

    def copy(self, i, j, index, dim, step):
        ref = self.buf.at[self.slot(i, j), self.at]
        return remote(ref, ref, self.sent.at[self.unit, index], self.landed.at[self.unit, index],
                      self.plane.devices[dim, step])

    def send(self, i, j, index, dim, step):
        copy = self.copy(i, j, index, dim, step)
        copy.start()
        self.started.append(copy)

    def await_first(self, index):
        self.copy((-1, 1, 2)[index], 0, index, self.dims[0], 1).wait_recv()

    def await_second(self, k, index):
        self.copy(OFFSETS[k], (-1, 1, 2)[index], 3 + 3 * k + index, self.dims[1], 1).wait_recv()

    def out_first(self):
        self.send(0, 0, 0, self.dims[0], 1)
        self.send(0, 0, 1, self.dims[0], -1)
        if "first" in self.opposite:
            self.send(0, 0, 2, self.dims[0], 2)

    def out_second(self, k):
        self.send(OFFSETS[k], 0, 3 + 3 * k, self.dims[1], 1)
        self.send(OFFSETS[k], 0, 4 + 3 * k, self.dims[1], -1)
        if k in self.opposite:
            self.send(OFFSETS[k], 0, 5 + 3 * k, self.dims[1], 2)

    def on_first(self):
        way = 1 if self.unit // 2 % 2 == 0 else -1
        order = ((0, -1, 1), (1, 1, 2)) if way == 1 else ((1, 1, 2), (0, -1, 1))
        for turn, (index, i, k) in enumerate(order):
            self.await_first(index)
            if turn == 0 and "first" not in self.opposite:
                self.send(i, 0, 2, self.dims[0], way)
            self.out_second(k)

    def far_first(self):
        self.await_first(2)
        self.out_second(3)

    def on_second(self, k):
        way = 1 if (self.unit // 2 + k) % 2 == 1 else -1
        order = (0, 1) if way == 1 else (1, 0)
        for turn, index in enumerate(order):
            self.await_second(k, index)
            if turn == 0 and k not in self.opposite:
                self.send(OFFSETS[k], -way, 5 + 3 * k, self.dims[1], way)

    def far_second(self, k):
        self.await_second(k, 2)

    def finish(self):
        for copy in self.started:
            copy.wait_send()


def run_units(units, multiply):
    def each(act, *args):
        for unit in units:
            act(unit, *args)

    each(Gather.out_first)
    each(Gather.out_second, 0)
    each(multiply, [(0, 0)])
    each(Gather.on_first)
    each(multiply, [(-1, 0), (1, 0)])
    each(Gather.on_second, 0)
    each(Gather.far_first)
    each(multiply, [(0, -1), (0, 1), (2, 0)])
    for k in (1, 2):
        each(Gather.on_second, k)
    each(multiply, [(i, j) for i in (-1, 1) for j in (-1, 1)])
    each(Gather.on_second, 3)
    each(multiply, [(2, -1), (2, 1)])
    for k in range(SIDE):
        for unit in units:
            unit.far_second(k)
            multiply(unit, [(OFFSETS[k], 2)])


def summed_over_plane(plane, own, column, line, sent, landed):
    steps = (1, -1, 2)
    total = own[...]
    copies = []
    for turn, (source, box, dim) in enumerate(((own, column, "y"), (line.at[3], line, "x"))):
        if turn == 1:
            line[3] = total
        turn_copies = []
        for at, step in enumerate(steps):
            index = 3 * turn + at
            copy = remote(source, box.at[at], sent.at[index], landed.at[index], plane.devices[dim, step])
            copy.start()
            turn_copies.append(copy)
        for copy in turn_copies:
            copy.wait_recv()
        for at in range(3):
            total = total + box[at]
        copies += turn_copies
    return total, copies


def make_units(plane, buf, sent, landed, rows, count, opposite):
    size = rows // count
    return [
        Gather(plane, buf, sent, landed, u, u * size, size, "yx" if u % 2 == 0 else "xy", opposite)
        for u in range(count)
    ]


SPAN = 4
NORM_ROWS = 16
IN_UNITS, OUT_UNITS = 4, 2
FACTOR = float(HD ** -0.5 * 1.4426950408889634)


def feat(u):
    return jnp.where(u > 0, u + 1.0, jnp.exp(jnp.minimum(u, 0.0)))


def product_of(buf, w_ref, acc, finish=None):
    begun, seen = set(), {}

    def multiply(unit, blocks):
        total = acc[unit.at] if unit.unit in begun else None
        for i, j in blocks:
            slot = unit.slot(i, j)
            term = jnp.dot(buf[slot, unit.at], w_ref[slot], preferred_element_type=F32)
            total = term if total is None else total + term
        begun.add(unit.unit)
        seen[unit.unit] = seen.get(unit.unit, 0) + len(blocks)
        if finish is not None and seen[unit.unit] == HEADS:
            finish(unit.at, total)
        else:
            acc[unit.at] = total

    return multiply


def layer_kernel(segments, gate_ref, tokens_hbm, gain_hbm, w_hbm, wo_hbm, o_ref,
                 tokens_ref, gain_ref, w_ref, wo_ref, buf, acc, own, column, line, q_ref, kv, top_ref, sum_ref, local_ref,
                 term, parts, outgoing, incoming, share, memory, obuf, oacc,
                 in_sem, g_sent, g_landed, n_sent, n_landed, kv_sent, kv_landed, a_sent, a_landed, b_sent, b_landed,
                 c_sent, c_landed, o_sent, o_landed):
    loads = [
        pltpu.make_async_copy(source, target, in_sem.at[at])
        for at, (source, target) in enumerate(
            ((tokens_hbm, tokens_ref), (gain_hbm, gain_ref), (w_hbm, w_ref), (wo_hbm, wo_ref))
        )
    ]
    for load in loads:
        load.start()
    plane = Plane()
    s, x, y = place()
    h = x * SIDE + y
    seg, pos = s // SPAN, s % SPAN
    base = seg * SPAN
    peers = {step: (base + lax.rem(pos + step, SPAN), h) for step in (1, 2, 3)}
    mate = (base + pos // 2 * 2 + 1 - pos % 2, h)
    mate_slot = pos // 2 * 2 + 1 - pos % 2
    across, across_slot = peers[2], lax.rem(pos + 2, SPAN)
    relayed_slot = lax.rem(mate_slot + 2, SPAN)
    later = [(lax.rem(s + SPAN * d, segments * SPAN), h) for d in range(1, segments)]
    partners = plane.neighbours() + [plane.devices["x", 2], plane.devices["y", 2]] + list(peers.values()) + later
    barrier = pltpu.get_barrier_semaphore()
    for partner in partners:
        pl.semaphore_signal(barrier, inc=1, device_id=partner, device_id_type=MESH)

    loads[0].wait()
    loads[1].wait()
    values = tokens_ref[...].astype(F32)
    rows, width = values.shape
    buf[h] = (values * gain_ref[...].astype(F32)).astype(BF16)
    own[...] = lax.dot_general(
        jnp.ones((8, width), F32), values * values, (((1,), (1,)), ((), ())),
        precision=HIGH, preferred_element_type=F32,
    )
    pl.semaphore_wait(barrier, len(partners))
    loads[2].wait()
    units = make_units(plane, buf, g_sent, g_landed, rows, IN_UNITS, ())
    run_units(units, product_of(buf, w_ref, acc))

    squares, norm_copies = summed_over_plane(plane, own, column, line, n_sent, n_landed)
    scale = lax.rsqrt(squares / (width * HEADS) + EPS)
    pick = (lax.broadcasted_iota(jnp.int32, (8, HD), 0) == 0).astype(F32)
    spread = lax.dot_general(scale, pick, (((0,), (0,)), ((), ())), precision=HIGH, preferred_element_type=F32)
    keys = (acc[:, HD : 2 * HD] * spread).astype(BF16)
    worth = (acc[:, 2 * HD :] * spread).astype(BF16)
    kv[pos, :, :HD] = keys
    kv[pos, :, HD:] = worth

    mine, theirs = kv.at[pos], kv.at[across_slot]
    to_across = remote(mine, mine, kv_sent.at[0], kv_landed.at[0], across)
    to_mate = remote(mine, mine, kv_sent.at[1], kv_landed.at[1], mate)
    relay = remote(theirs, theirs, kv_sent.at[2], kv_landed.at[2], mate)
    from_across = remote(theirs, theirs, kv_sent.at[0], kv_landed.at[0], across)
    from_mate = remote(kv.at[mate_slot], kv.at[mate_slot], kv_sent.at[1], kv_landed.at[1], mate)
    from_relay = remote(kv.at[relayed_slot], kv.at[relayed_slot], kv_sent.at[2], kv_landed.at[2], mate)

    piece = HD // SPAN
    keys = feat(keys.astype(F32))
    term[:HD] = lax.dot_general(
        keys.astype(BF16), worth, (((0,), (0,)), ((), ())), preferred_element_type=F32
    ).astype(BF16)
    term[HD:] = jnp.broadcast_to(jnp.sum(keys, axis=0, keepdims=True), (NORM_ROWS, HD)).astype(BF16)
    first = []
    for step in (1, 2, 3):
        to = lax.rem(pos + step, SPAN)
        for at, (lo, size, low) in enumerate(((to * piece, piece, 0), (HD, NORM_ROWS, piece))):
            index = 2 * (step - 1) + at
            copy = remote(term.at[pl.ds(pl.multiple_of(lo, 16), size)], parts.at[step - 1, pl.ds(low, size)],
                          a_sent.at[index], a_landed.at[index], peers[step])
            copy.start()
            first.append(copy)
    to_across.start()
    to_mate.start()
    q_ref[...] = (acc[:, :HD] * spread).astype(BF16)
    for copy in first:
        copy.wait_recv()
    here = pl.ds(pl.multiple_of(pos * piece, 16), piece)
    total = jnp.concatenate([term[here], term[HD:]], axis=0).astype(F32)
    for at in range(3):
        total = total + parts[at].astype(F32)
    outgoing[...] = total.astype(BF16)

    def second(d):
        return remote(outgoing, incoming.at[d - 1], b_sent.at[d - 1], b_landed.at[d - 1], later[d - 1])

    order = sorted(range(1, segments), key=lambda d: -min(d, segments - d))
    for d in order:
        @pl.when(seg + d < segments)
        def _():
            second(d).start()

    chunk = 128

    def attend(slot, causal):
        for r in range(rows // chunk):
            at = pl.ds(r * chunk, chunk)
            live = (r + 1) * chunk if causal else rows
            scores = lax.dot_general(
                q_ref[at], kv[slot, :live, :HD], (((1,), (1,)), ((), ())), preferred_element_type=F32
            )
            if causal:
                row = lax.broadcasted_iota(jnp.int32, (chunk, live), 0) + r * chunk
                scores = jnp.where(row >= lax.broadcasted_iota(jnp.int32, (chunk, live), 1), scores, -1e30)
            top = jnp.max(scores, axis=1, keepdims=True)
            if not causal:
                before = top_ref[at]
                top = jnp.maximum(top, before)
                shrink = jnp.exp2((before - top) * FACTOR)
            expo = jnp.exp2((scores - top) * FACTOR)
            weight = jnp.sum(expo, axis=1, keepdims=True)
            mixed = jnp.dot(expo.astype(BF16), kv[slot, :live, HD:], preferred_element_type=F32)
            if not causal:
                weight = weight + sum_ref[at] * shrink
                mixed = mixed + local_ref[at] * shrink
            top_ref[at] = top
            sum_ref[at] = weight
            local_ref[at] = mixed

    attend(pos, True)
    from_mate.wait_recv()

    @pl.when(mate_slot < pos)
    def _():
        attend(mate_slot, False)

    from_across.wait_recv()
    relay.start()

    @pl.when(across_slot < pos)
    def _():
        attend(across_slot, False)

    from_relay.wait_recv()

    @pl.when(relayed_slot < pos)
    def _():
        attend(relayed_slot, False)

    gate = jax.nn.sigmoid(jnp.full((1, HD), gate_ref[0], F32))
    local_ref[...] = local_ref[...] * ((1.0 - gate) / sum_ref[...])
    queries = feat(q_ref[...].astype(F32))

    share[...] = jnp.zeros_like(share)
    for d in reversed(order):
        @pl.when(seg - d >= 0)
        def _():
            second(d).wait_recv()
            share[...] += incoming[d - 1].astype(F32)
    memory[here] = share[:piece].astype(BF16)
    third = []
    for step in (1, 2, 3):
        copy = remote(memory.at[here], memory.at[here], c_sent.at[step - 1], c_landed.at[step - 1], peers[step])
        copy.start()
        third.append(copy)
    denom = jnp.maximum(jnp.sum(queries * share[piece : piece + 1], axis=1, keepdims=True), 1.0)
    for step in (1, 2, 3):
        there = memory.at[pl.ds(pl.multiple_of(lax.rem(pos + SPAN - step, SPAN) * piece, 16), piece)]
        remote(there, there, c_sent.at[step - 1], c_landed.at[step - 1], peers[step]).wait_recv()
    numer = jnp.dot(queries.astype(BF16), memory[...], preferred_element_type=F32)
    obuf[h] = (numer * (gate / denom) + local_ref[...]).astype(BF16)

    loads[3].wait()
    out_units = make_units(plane, obuf, o_sent, o_landed, rows, OUT_UNITS, ("first", 3))

    def finish(at, total):
        o_ref[at] = total.astype(BF16)

    run_units(out_units, product_of(obuf, wo_ref, oacc, finish))

    for unit in units + out_units:
        unit.finish()
    for copy in [to_across, to_mate, relay] + first + third + norm_copies:
        copy.wait_send()
    for d in order:
        @pl.when(seg + d < segments)
        def _():
            second(d).wait_send()


def layer(gate, tokens, gain, weights, out_weights, segments):
    rows, width = tokens.shape
    columns, out_columns = weights.shape[2], out_weights.shape[2]
    piece = HD // SPAN
    anywhere = pl.BlockSpec(memory_space=pl.ANY)
    dma = pltpu.SemaphoreType.DMA
    return pl.pallas_call(
        functools.partial(layer_kernel, segments),
        out_shape=jax.ShapeDtypeStruct((rows, out_columns), BF16),
        in_specs=[pl.BlockSpec(memory_space=pltpu.SMEM)] + [anywhere] * 4,
        out_specs=pl.BlockSpec(memory_space=pltpu.VMEM),
        scratch_shapes=[
            pltpu.VMEM((rows, width), BF16),
            pltpu.VMEM((1, width), BF16),
            pltpu.VMEM((HEADS, width, columns), BF16),
            pltpu.VMEM((HEADS, HD, out_columns), BF16),
            pltpu.VMEM((HEADS, rows, width), BF16),
            pltpu.VMEM((rows, columns), F32),
            pltpu.VMEM((8, rows), F32),
            pltpu.VMEM((3, 8, rows), F32),
            pltpu.VMEM((4, 8, rows), F32),
            pltpu.VMEM((rows, HD), BF16),
            pltpu.VMEM((SPAN, rows, 2 * HD), BF16),
            pltpu.VMEM((rows, 1), F32),
            pltpu.VMEM((rows, 1), F32),
            pltpu.VMEM((rows, HD), F32),
            pltpu.VMEM((HD + NORM_ROWS, HD), BF16),
            pltpu.VMEM((3, piece + NORM_ROWS, HD), BF16),
            pltpu.VMEM((piece + NORM_ROWS, HD), BF16),
            pltpu.VMEM((segments - 1, piece + NORM_ROWS, HD), BF16),
            pltpu.VMEM((piece + NORM_ROWS, HD), F32),
            pltpu.VMEM((HD, HD), BF16),
            pltpu.VMEM((HEADS, rows, HD), BF16),
            pltpu.VMEM((rows, out_columns), F32),
            dma((4,)),
            dma((IN_UNITS, 15)),
            dma((IN_UNITS, 15)),
            dma((6,)),
            dma((6,)),
            dma((3,)),
            dma((3,)),
            dma((6,)),
            dma((6,)),
            dma((segments - 1,)),
            dma((segments - 1,)),
            dma((3,)),
            dma((3,)),
            dma((OUT_UNITS, 15)),
            dma((OUT_UNITS, 15)),
        ],
        compiler_params=pltpu.CompilerParams(collective_id=0, has_side_effects=True, vmem_limit_bytes=56 << 20),
        name="layer",
    )(gate, tokens, gain, weights, out_weights)


def on_device(tokens, norm_gain, qkv_weight, out_weight, mem_gate):
    weights = qkv_weight.reshape(HEADS, tokens.shape[1], 3 * HD)
    out_weights = out_weight.reshape(HEADS, HD, out_weight.shape[1])
    return layer(mem_gate, tokens, norm_gain, weights, out_weights, lax.axis_size("seq") // SPAN)


def solution(mesh):
    placed = (P("seq", "head"), P(None, "head"), P(None, "head", None), P(None, "head"), P("head"))
    return jax.shard_map(
        on_device, mesh=mesh, in_specs=placed, out_specs=P("seq", "head"), check_vma=False
    )
```

time: 276 us -> 81.5 us (0.30)
  the two profiles are of different devices: /device:TPU:1 before, /device:TPU:2 now
where the time goes in v2:
time: 81.5 us; the launch traced here: 81.4 us
  Pallas kernels  79.1 us (97%)
  local copies, waits for them, and re-layouts  1.67 us (2%)
    pallas_call x1, Pallas kernels, layer(): pl.pallas_call(functools.partial(layer_kernel, segments), out_shape=jax.S...  79.1 us
    unnamed x1, local copies, waits for them, and re-layouts  1.67 us

profile of v2, /device:TPU:2, one launch (start us, length us, event | category | flops | bytes accessed | tf_op | source)
XLA Modules:
  0.0 81.4 jit_solution(314387877187208238)
XLA Ops:
  0.7 79.1 %layer.1 = bf16[512,256]{1,0:T(8,128)(2,1)} custom-call(f32[1]{0:T(128)S(6)} %copy.7.gate_ref, bf16[512,256]{1,0:T(8,128)(2,1)} %tokens_hbm.1, bf16[1,256]{1,0:T(2,128)(2,1)} %gain_hbm.1, bf16[16,256,384]{2,1,0:T(8,128)(2,1)} %bitcast.2, bf16[16,128,256]{2,1,0:T(8,128)(2,1)} %bitcast.3), custom_call_target="tpu_custom_call" | custom-call | tf_op jit(solution)/shard_map/layer/pallas_call | solution.py:387
  79.7 1.7 %copy.8 = bf16[512,256]{1,0:T(8,128)(2,1)} copy(bf16[512,256]{1,0:T(8,128)(2,1)} %layer.1) | data formatting | bytes 524288

commit v3 on v2

--- a/solution.py
+++ b/solution.py
@@ -113,18 +113,27 @@
             copy.wait_send()
 
 
-def run_units(units, multiply):
+def run_units(units, multiply, between=()):
+    between = list(between)
+
     def each(act, *args):
         for unit in units:
             act(unit, *args)
 
+    def aside():
+        if between:
+            between.pop(0)()
+
     each(Gather.out_first)
     each(Gather.out_second, 0)
+    aside()
     each(multiply, [(0, 0)])
     each(Gather.on_first)
+    aside()
     each(multiply, [(-1, 0), (1, 0)])
     each(Gather.on_second, 0)
     each(Gather.far_first)
+    aside()
     each(multiply, [(0, -1), (0, 1), (2, 0)])
     for k in (1, 2):
         each(Gather.on_second, k)
@@ -137,25 +146,32 @@
             multiply(unit, [(OFFSETS[k], 2)])
 
 
-def summed_over_plane(plane, own, column, line, sent, landed):
-    steps = (1, -1, 2)
-    total = own[...]
-    copies = []
-    for turn, (source, box, dim) in enumerate(((own, column, "y"), (line.at[3], line, "x"))):
-        if turn == 1:
-            line[3] = total
-        turn_copies = []
-        for at, step in enumerate(steps):
+class PlaneSum:
+    def __init__(self, plane, own, column, line, sent, landed):
+        self.plane, self.boxes, self.sent, self.landed = plane, (column, line), sent, landed
+        self.sources, self.copies = (own, line.at[3]), []
+
+    def start(self, turn):
+        for at, step in enumerate((1, -1, 2)):
             index = 3 * turn + at
-            copy = remote(source, box.at[at], sent.at[index], landed.at[index], plane.devices[dim, step])
+            copy = remote(self.sources[turn], self.boxes[turn].at[at], self.sent.at[index], self.landed.at[index],
+                          self.plane.devices["yx"[turn], step])
             copy.start()
-            turn_copies.append(copy)
-        for copy in turn_copies:
+            self.copies.append(copy)
+
+    def total(self, turn):
+        for copy in self.copies[3 * turn :]:
             copy.wait_recv()
-        for at in range(3):
-            total = total + box[at]
-        copies += turn_copies
-    return total, copies
+        box = self.boxes[turn]
+        return self.sources[turn][...] + box[0] + box[1] + box[2]
+
+    def pass_on(self):
+        self.boxes[1][3] = self.total(0)
+        self.start(1)
+
+    def finish(self):
+        for copy in self.copies:
+            copy.wait_send()
 
 
 def make_units(plane, buf, sent, landed, rows, count, opposite):
@@ -196,9 +212,9 @@
 
 
 def layer_kernel(segments, gate_ref, tokens_hbm, gain_hbm, w_hbm, wo_hbm, o_ref,
-                 tokens_ref, gain_ref, w_ref, wo_ref, buf, acc, own, column, line, q_ref, kv, top_ref, sum_ref, local_ref,
+                 tokens_ref, gain_ref, w_ref, wo_ref, buf, acc, own, column, line, spread, q_ref, kv, top_ref, sum_ref, local_ref,
                  term, parts, outgoing, incoming, share, memory, obuf, oacc,
-                 in_sem, g_sent, g_landed, n_sent, n_landed, kv_sent, kv_landed, a_sent, a_landed, b_sent, b_landed,
+                 ready, in_sem, g_sent, g_landed, n_sent, n_landed, kv_sent, kv_landed, a_sent, a_landed, b_sent, b_landed,
                  c_sent, c_landed, o_sent, o_landed):
     loads = [
         pltpu.make_async_copy(source, target, in_sem.at[at])
@@ -219,7 +235,7 @@
     across, across_slot = peers[2], lax.rem(pos + 2, SPAN)
     relayed_slot = lax.rem(mate_slot + 2, SPAN)
     later = [(lax.rem(s + SPAN * d, segments * SPAN), h) for d in range(1, segments)]
-    partners = plane.neighbours() + [plane.devices["x", 2], plane.devices["y", 2]] + list(peers.values()) + later
+    partners = plane.neighbours() + [plane.devices["x", 2], plane.devices["y", 2]] + list(peers.values()) + [later[0], later[-1]]
     barrier = pltpu.get_barrier_semaphore()
     for partner in partners:
         pl.semaphore_signal(barrier, inc=1, device_id=partner, device_id_type=MESH)
@@ -235,17 +251,53 @@
     )
     pl.semaphore_wait(barrier, len(partners))
     loads[2].wait()
+    squares = PlaneSum(plane, own, column, line, n_sent, n_landed)
+    squares.start(0)
+
+    def scales():
+        scale = lax.rsqrt(squares.total(1) / (width * HEADS) + EPS)
+        pick = (lax.broadcasted_iota(jnp.int32, (8, HD), 0) == 0).astype(F32)
+        spread[...] = lax.dot_general(
+            scale, pick, (((0,), (0,)), ((), ())), precision=HIGH, preferred_element_type=F32
+        )
+
+    piece = HD // SPAN
+    whole = []
+
+    def finish_rows(at, total):
+        rscale = spread[at]
+        key = (total[:, HD : 2 * HD] * rscale).astype(BF16)
+        value = (total[:, 2 * HD :] * rscale).astype(BF16)
+        kv[pos, at, :HD] = key
+        kv[pos, at, HD:] = value
+        key = feat(key.astype(F32))
+        product = lax.dot_general(key.astype(BF16), value, (((0,), (0,)), ((), ())), preferred_element_type=F32)
+        amount = jnp.sum(key, axis=0, keepdims=True)
+        whole[:] = [whole[0] + product, whole[1] + amount] if whole else [product, amount]
+        q_ref[at] = (total[:, :HD] * rscale).astype(BF16)
+
+    def tell(turn):
+        pl.semaphore_signal(ready.at[turn, 0], inc=1, device_id=later[0], device_id_type=MESH)
+        pl.semaphore_signal(ready.at[turn, 1], inc=1, device_id=later[-1], device_id_type=MESH)
+
+    def hear(turn):
+        pl.semaphore_wait(ready.at[turn, 0], 1)
+        pl.semaphore_wait(ready.at[turn, 1], 1)
+
+    tell(0)
+
+    def early():
+        squares.pass_on()
+        hear(0)
+        tell(1)
+
+    def late():
+        scales()
+        hear(1)
+        tell(2)
+
     units = make_units(plane, buf, g_sent, g_landed, rows, IN_UNITS, ())
-    run_units(units, product_of(buf, w_ref, acc))
-
-    squares, norm_copies = summed_over_plane(plane, own, column, line, n_sent, n_landed)
-    scale = lax.rsqrt(squares / (width * HEADS) + EPS)
-    pick = (lax.broadcasted_iota(jnp.int32, (8, HD), 0) == 0).astype(F32)
-    spread = lax.dot_general(scale, pick, (((0,), (0,)), ((), ())), precision=HIGH, preferred_element_type=F32)
-    keys = (acc[:, HD : 2 * HD] * spread).astype(BF16)
-    worth = (acc[:, 2 * HD :] * spread).astype(BF16)
-    kv[pos, :, :HD] = keys
-    kv[pos, :, HD:] = worth
+    run_units(units, product_of(buf, w_ref, acc, finish_rows), (lambda: None, early, late))
 
     mine, theirs = kv.at[pos], kv.at[across_slot]
     to_across = remote(mine, mine, kv_sent.at[0], kv_landed.at[0], across)
@@ -255,28 +307,25 @@
     from_mate = remote(kv.at[mate_slot], kv.at[mate_slot], kv_sent.at[1], kv_landed.at[1], mate)
     from_relay = remote(kv.at[relayed_slot], kv.at[relayed_slot], kv_sent.at[2], kv_landed.at[2], mate)
 
-    piece = HD // SPAN
-    keys = feat(keys.astype(F32))
-    term[:HD] = lax.dot_general(
-        keys.astype(BF16), worth, (((0,), (0,)), ((), ())), preferred_element_type=F32
-    ).astype(BF16)
-    term[HD:] = jnp.broadcast_to(jnp.sum(keys, axis=0, keepdims=True), (NORM_ROWS, HD)).astype(BF16)
+    for at in range(SPAN):
+        term[at, :piece] = whole[0][at * piece : (at + 1) * piece].astype(BF16)
+        term[at, piece:] = jnp.broadcast_to(whole[1], (NORM_ROWS, HD)).astype(BF16)
     first = []
-    for step in (1, 2, 3):
-        to = lax.rem(pos + step, SPAN)
-        for at, (lo, size, low) in enumerate(((to * piece, piece, 0), (HD, NORM_ROWS, piece))):
-            index = 2 * (step - 1) + at
-            copy = remote(term.at[pl.ds(pl.multiple_of(lo, 16), size)], parts.at[step - 1, pl.ds(low, size)],
-                          a_sent.at[index], a_landed.at[index], peers[step])
-            copy.start()
-            first.append(copy)
-    to_across.start()
+    for step in (2, 1, 3):
+        copy = remote(term.at[lax.rem(pos + step, SPAN)], parts.at[step - 1],
+                      a_sent.at[step - 1], a_landed.at[step - 1], peers[step])
+        copy.start()
+        first.append(copy)
+
+    @pl.when(pos < 2)
+    def _():
+        to_across.start()
+
     to_mate.start()
-    q_ref[...] = (acc[:, :HD] * spread).astype(BF16)
     for copy in first:
         copy.wait_recv()
     here = pl.ds(pl.multiple_of(pos * piece, 16), piece)
-    total = jnp.concatenate([term[here], term[HD:]], axis=0).astype(F32)
+    total = term[pos].astype(F32)
     for at in range(3):
         total = total + parts[at].astype(F32)
     outgoing[...] = total.astype(BF16)
@@ -284,6 +333,7 @@
     def second(d):
         return remote(outgoing, incoming.at[d - 1], b_sent.at[d - 1], b_landed.at[d - 1], later[d - 1])
 
+    hear(2)
     order = sorted(range(1, segments), key=lambda d: -min(d, segments - d))
     for d in order:
         @pl.when(seg + d < segments)
@@ -324,17 +374,12 @@
     def _():
         attend(mate_slot, False)
 
-    from_across.wait_recv()
-    relay.start()
-
-    @pl.when(across_slot < pos)
+    @pl.when(pos >= 2)
     def _():
+        from_across.wait_recv()
+        relay.start()
         attend(across_slot, False)
-
-    from_relay.wait_recv()
-
-    @pl.when(relayed_slot < pos)
-    def _():
+        from_relay.wait_recv()
         attend(relayed_slot, False)
 
     gate = jax.nn.sigmoid(jnp.full((1, HD), gate_ref[0], F32))
@@ -370,8 +415,18 @@
 
     for unit in units + out_units:
         unit.finish()
-    for copy in [to_across, to_mate, relay] + first + third + norm_copies:
+    squares.finish()
+    for copy in [to_mate] + first + third:
         copy.wait_send()
+
+    @pl.when(pos < 2)
+    def _():
+        to_across.wait_send()
+
+    @pl.when(pos >= 2)
+    def _():
+        relay.wait_send()
+
     for d in order:
         @pl.when(seg + d < segments)
         def _():
@@ -399,12 +454,13 @@
             pltpu.VMEM((8, rows), F32),
             pltpu.VMEM((3, 8, rows), F32),
             pltpu.VMEM((4, 8, rows), F32),
+            pltpu.VMEM((rows, HD), F32),
             pltpu.VMEM((rows, HD), BF16),
             pltpu.VMEM((SPAN, rows, 2 * HD), BF16),
             pltpu.VMEM((rows, 1), F32),
             pltpu.VMEM((rows, 1), F32),
             pltpu.VMEM((rows, HD), F32),
-            pltpu.VMEM((HD + NORM_ROWS, HD), BF16),
+            pltpu.VMEM((SPAN, piece + NORM_ROWS, HD), BF16),
             pltpu.VMEM((3, piece + NORM_ROWS, HD), BF16),
             pltpu.VMEM((piece + NORM_ROWS, HD), BF16),
             pltpu.VMEM((segments - 1, piece + NORM_ROWS, HD), BF16),
@@ -412,6 +468,7 @@
             pltpu.VMEM((HD, HD), BF16),
             pltpu.VMEM((HEADS, rows, HD), BF16),
             pltpu.VMEM((rows, out_columns), F32),
+            pltpu.SemaphoreType.REGULAR((3, 2)),
             dma((4,)),
             dma((IN_UNITS, 15)),
             dma((IN_UNITS, 15)),
@@ -419,8 +476,8 @@
             dma((6,)),
             dma((3,)),
             dma((3,)),
-            dma((6,)),
-            dma((6,)),
+            dma((3,)),
+            dma((3,)),
             dma((segments - 1,)),
             dma((segments - 1,)),
             dma((3,)),

time: 81.5 us -> 72 us (0.88)
  the two profiles are of different devices: /device:TPU:2 before, /device:TPU:16 now
where the time goes in v3:
time: 72 us; the launch traced here: 71.8 us
  Pallas kernels  69.5 us (97%)
  local copies, waits for them, and re-layouts  1.67 us (2%)
    pallas_call x1, Pallas kernels, layer(): pl.pallas_call(functools.partial(layer_kernel, segments), out_shape=jax.S...  69.5 us
    unnamed x1, local copies, waits for them, and re-layouts  1.67 us

profile of v3, /device:TPU:16, one launch (start us, length us, event | category | flops | bytes accessed | tf_op | source)
XLA Modules:
  0.0 71.8 jit_solution(18420824528760589546)
XLA Ops:
  0.7 69.5 %layer.1 = bf16[512,256]{1,0:T(8,128)(2,1)} custom-call(f32[1]{0:T(128)S(6)} %copy.7.gate_ref, bf16[512,256]{1,0:T(8,128)(2,1)} %tokens_hbm.1, bf16[1,256]{1,0:T(2,128)(2,1)} %gain_hbm.1, bf16[16,256,384]{2,1,0:T(8,128)(2,1)} %bitcast.2, bf16[16,128,256]{2,1,0:T(8,128)(2,1)} %bitcast.3), custom_call_target="tpu_custom_call" | custom-call | tf_op jit(solution)/shard_map/layer/pallas_call | solution.py:442
  70.2 1.7 %copy.8 = bf16[512,256]{1,0:T(8,128)(2,1)} copy(bf16[512,256]{1,0:T(8,128)(2,1)} %layer.1) | data formatting | bytes 524288

commit v4 on v3

--- a/solution.py
+++ b/solution.py
@@ -50,7 +50,8 @@
 class Gather:
     def __init__(self, plane, buf, sent, landed, unit, first_row, rows, dims, opposite):
         self.plane, self.buf, self.sent, self.landed, self.unit = plane, buf, sent, landed, unit
-        self.at, self.dims, self.opposite = pl.ds(first_row, rows), dims, opposite
+        self.lo, self.rows, self.dims, self.opposite = first_row, rows, dims, opposite
+        self.at = pl.ds(first_row, rows)
         self.started = []
 
     def slot(self, i, j):
@@ -85,7 +86,7 @@
             self.send(OFFSETS[k], 0, 5 + 3 * k, self.dims[1], 2)
 
     def on_first(self):
-        way = 1 if self.unit // 2 % 2 == 0 else -1
+        way = 1 if self.unit % 2 == 0 else -1
         order = ((0, -1, 1), (1, 1, 2)) if way == 1 else ((1, 1, 2), (0, -1, 1))
         for turn, (index, i, k) in enumerate(order):
             self.await_first(index)
@@ -98,7 +99,7 @@
         self.out_second(3)
 
     def on_second(self, k):
-        way = 1 if (self.unit // 2 + k) % 2 == 1 else -1
+        way = 1 if (self.unit + k) % 2 == 1 else -1
         order = (0, 1) if way == 1 else (1, 0)
         for turn, index in enumerate(order):
             self.await_second(k, index)
@@ -115,10 +116,18 @@
 
 def run_units(units, multiply, between=()):
     between = list(between)
+    half = len(units) // 2
+    groups = [units[:half], units[half:]]
 
     def each(act, *args):
-        for unit in units:
-            act(unit, *args)
+        for at in range(half):
+            for group in groups:
+                act(group[at], *args)
+
+    def product(blocks):
+        for group in groups:
+            for unit in group:
+                multiply([unit], blocks)
 
     def aside():
         if between:
@@ -127,23 +136,30 @@
     each(Gather.out_first)
     each(Gather.out_second, 0)
     aside()
-    each(multiply, [(0, 0)])
+    product([(0, 0)])
     each(Gather.on_first)
     aside()
-    each(multiply, [(-1, 0), (1, 0)])
+    product([(-1, 0), (1, 0)])
     each(Gather.on_second, 0)
     each(Gather.far_first)
     aside()
-    each(multiply, [(0, -1), (0, 1), (2, 0)])
+    product([(0, -1), (0, 1), (2, 0)])
+    aside()
     for k in (1, 2):
         each(Gather.on_second, k)
-    each(multiply, [(i, j) for i in (-1, 1) for j in (-1, 1)])
+    product([(i, j) for i in (-1, 1) for j in (-1, 1)])
+    aside()
     each(Gather.on_second, 3)
-    each(multiply, [(2, -1), (2, 1)])
-    for k in range(SIDE):
-        for unit in units:
-            unit.far_second(k)
-            multiply(unit, [(OFFSETS[k], 2)])
+    product([(2, -1), (2, 1)])
+    aside()
+    for k in range(SIDE - 1):
+        each(Gather.far_second, k)
+        product([(OFFSETS[k], 2)])
+        aside()
+    for at in range(half):
+        for group in groups:
+            group[at].far_second(SIDE - 1)
+            multiply([group[at]], [(OFFSETS[SIDE - 1], 2)])
 
 
 class PlaneSum:
@@ -177,7 +193,7 @@
 def make_units(plane, buf, sent, landed, rows, count, opposite):
     size = rows // count
     return [
-        Gather(plane, buf, sent, landed, u, u * size, size, "yx" if u % 2 == 0 else "xy", opposite)
+        Gather(plane, buf, sent, landed, u, u * size, size, "yx" if u < count // 2 else "xy", opposite)
         for u in range(count)
     ]
 
@@ -195,18 +211,21 @@
 def product_of(buf, w_ref, acc, finish=None):
     begun, seen = set(), {}
 
-    def multiply(unit, blocks):
-        total = acc[unit.at] if unit.unit in begun else None
+    def multiply(units, blocks):
+        at = pl.ds(units[0].lo, sum(unit.rows for unit in units))
+        key = tuple(unit.unit for unit in units)
+        total = acc[at] if begun.issuperset(key) else None
         for i, j in blocks:
-            slot = unit.slot(i, j)
-            term = jnp.dot(buf[slot, unit.at], w_ref[slot], preferred_element_type=F32)
+            slot = units[0].slot(i, j)
+            term = jnp.dot(buf[slot, at], w_ref[slot], preferred_element_type=F32)
             total = term if total is None else total + term
-        begun.add(unit.unit)
-        seen[unit.unit] = seen.get(unit.unit, 0) + len(blocks)
-        if finish is not None and seen[unit.unit] == HEADS:
-            finish(unit.at, total)
+        begun.update(key)
+        for one in key:
+            seen[one] = seen.get(one, 0) + len(blocks)
+        if finish is not None and seen[key[0]] == HEADS:
+            finish(units[0], total)
         else:
-            acc[unit.at] = total
+            acc[at] = total
 
     return multiply
 
@@ -235,10 +254,15 @@
     across, across_slot = peers[2], lax.rem(pos + 2, SPAN)
     relayed_slot = lax.rem(mate_slot + 2, SPAN)
     later = [(lax.rem(s + SPAN * d, segments * SPAN), h) for d in range(1, segments)]
-    partners = plane.neighbours() + [plane.devices["x", 2], plane.devices["y", 2]] + list(peers.values()) + [later[0], later[-1]]
+    partners = plane.neighbours() + [plane.devices["x", 2], plane.devices["y", 2]] + list(peers.values())
     barrier = pltpu.get_barrier_semaphore()
     for partner in partners:
         pl.semaphore_signal(barrier, inc=1, device_id=partner, device_id_type=MESH)
+
+    for d in range(1, segments):
+        @pl.when(seg + d < segments)
+        def _():
+            pl.semaphore_signal(barrier, inc=1, device_id=later[d - 1], device_id_type=MESH)
 
     loads[0].wait()
     loads[1].wait()
@@ -249,10 +273,9 @@
         jnp.ones((8, width), F32), values * values, (((1,), (1,)), ((), ())),
         precision=HIGH, preferred_element_type=F32,
     )
-    pl.semaphore_wait(barrier, len(partners))
-    loads[2].wait()
+    pl.semaphore_wait(barrier, len(partners) + seg)
+
     squares = PlaneSum(plane, own, column, line, n_sent, n_landed)
-    squares.start(0)
 
     def scales():
         scale = lax.rsqrt(squares.total(1) / (width * HEADS) + EPS)
@@ -263,8 +286,20 @@
 
     piece = HD // SPAN
     whole = []
-
-    def finish_rows(at, total):
+    size = rows // IN_UNITS
+
+    def over(slot, unit, to):
+        ref = kv.at[slot, pl.ds(unit * size, size)]
+        return remote(ref, ref, kv_sent.at[1 + unit], kv_landed.at[1 + unit], to)
+
+    def relay(slot, unit):
+        ref = kv.at[slot, pl.ds(unit * size, size)]
+        at = 1 + IN_UNITS + unit
+        return remote(ref, ref, kv_sent.at[at], kv_landed.at[at], mate)
+
+
+    def finish_rows(unit, total):
+        at = unit.at
         rscale = spread[at]
         key = (total[:, HD : 2 * HD] * rscale).astype(BF16)
         value = (total[:, 2 * HD :] * rscale).astype(BF16)
@@ -276,36 +311,19 @@
         whole[:] = [whole[0] + product, whole[1] + amount] if whole else [product, amount]
         q_ref[at] = (total[:, :HD] * rscale).astype(BF16)
 
-    def tell(turn):
-        pl.semaphore_signal(ready.at[turn, 0], inc=1, device_id=later[0], device_id_type=MESH)
-        pl.semaphore_signal(ready.at[turn, 1], inc=1, device_id=later[-1], device_id_type=MESH)
-
-    def hear(turn):
-        pl.semaphore_wait(ready.at[turn, 0], 1)
-        pl.semaphore_wait(ready.at[turn, 1], 1)
-
-    tell(0)
-
-    def early():
-        squares.pass_on()
-        hear(0)
-        tell(1)
-
-    def late():
-        scales()
-        hear(1)
-        tell(2)
+    def begin():
+        squares.start(0)
+        loads[2].wait()
+        for d in range(1, segments):
+            @pl.when(seg - d >= 0)
+            def _():
+                pl.semaphore_signal(ready.at[d - 1], inc=1, device_id=later[segments - d - 1], device_id_type=MESH)
 
     units = make_units(plane, buf, g_sent, g_landed, rows, IN_UNITS, ())
-    run_units(units, product_of(buf, w_ref, acc, finish_rows), (lambda: None, early, late))
-
-    mine, theirs = kv.at[pos], kv.at[across_slot]
-    to_across = remote(mine, mine, kv_sent.at[0], kv_landed.at[0], across)
-    to_mate = remote(mine, mine, kv_sent.at[1], kv_landed.at[1], mate)
-    relay = remote(theirs, theirs, kv_sent.at[2], kv_landed.at[2], mate)
-    from_across = remote(theirs, theirs, kv_sent.at[0], kv_landed.at[0], across)
-    from_mate = remote(kv.at[mate_slot], kv.at[mate_slot], kv_sent.at[1], kv_landed.at[1], mate)
-    from_relay = remote(kv.at[relayed_slot], kv.at[relayed_slot], kv_sent.at[2], kv_landed.at[2], mate)
+    run_units(units, product_of(buf, w_ref, acc, finish_rows), [begin, squares.pass_on, scales])
+
+    to_mate = remote(kv.at[pos], kv.at[pos], kv_sent.at[0], kv_landed.at[0], mate)
+    from_mate = remote(kv.at[mate_slot], kv.at[mate_slot], kv_sent.at[0], kv_landed.at[0], mate)
 
     for at in range(SPAN):
         term[at, :piece] = whole[0][at * piece : (at + 1) * piece].astype(BF16)
@@ -319,7 +337,8 @@
 
     @pl.when(pos < 2)
     def _():
-        to_across.start()
+        for unit in range(IN_UNITS):
+            over(pos, unit, across).start()
 
     to_mate.start()
     for copy in first:
@@ -333,11 +352,11 @@
     def second(d):
         return remote(outgoing, incoming.at[d - 1], b_sent.at[d - 1], b_landed.at[d - 1], later[d - 1])
 
-    hear(2)
     order = sorted(range(1, segments), key=lambda d: -min(d, segments - d))
     for d in order:
         @pl.when(seg + d < segments)
         def _():
+            pl.semaphore_wait(ready.at[d - 1], 1)
             second(d).start()
 
     chunk = 128
@@ -376,15 +395,17 @@
 
     @pl.when(pos >= 2)
     def _():
-        from_across.wait_recv()
-        relay.start()
+        for unit in range(IN_UNITS):
+            over(across_slot, unit, across).wait_recv()
+            relay(across_slot, unit).start()
         attend(across_slot, False)
-        from_relay.wait_recv()
+        for unit in range(IN_UNITS):
+            relay(relayed_slot, unit).wait_recv()
         attend(relayed_slot, False)
 
     gate = jax.nn.sigmoid(jnp.full((1, HD), gate_ref[0], F32))
     local_ref[...] = local_ref[...] * ((1.0 - gate) / sum_ref[...])
-    queries = feat(q_ref[...].astype(F32))
+    queries = feat(q_ref[...].astype(F32)).astype(BF16)
 
     share[...] = jnp.zeros_like(share)
     for d in reversed(order):
@@ -398,18 +419,23 @@
         copy = remote(memory.at[here], memory.at[here], c_sent.at[step - 1], c_landed.at[step - 1], peers[step])
         copy.start()
         third.append(copy)
-    denom = jnp.maximum(jnp.sum(queries * share[piece : piece + 1], axis=1, keepdims=True), 1.0)
+    pick = (lax.broadcasted_iota(jnp.int32, (8, HD), 0) == 0).astype(F32)
+    norm = lax.dot_general(
+        share[piece : piece + 8], pick, (((0,), (0,)), ((), ())), precision=HIGH, preferred_element_type=F32
+    )
+    denom = jnp.dot(queries, norm.astype(BF16), preferred_element_type=F32)
+    weight = gate / jnp.maximum(denom, 1.0)
     for step in (1, 2, 3):
         there = memory.at[pl.ds(pl.multiple_of(lax.rem(pos + SPAN - step, SPAN) * piece, 16), piece)]
         remote(there, there, c_sent.at[step - 1], c_landed.at[step - 1], peers[step]).wait_recv()
-    numer = jnp.dot(queries.astype(BF16), memory[...], preferred_element_type=F32)
-    obuf[h] = (numer * (gate / denom) + local_ref[...]).astype(BF16)
+    numer = jnp.dot(queries, memory[...], preferred_element_type=F32)
+    obuf[h] = (numer * weight + local_ref[...]).astype(BF16)
 
     loads[3].wait()
-    out_units = make_units(plane, obuf, o_sent, o_landed, rows, OUT_UNITS, ("first", 3))
-
-    def finish(at, total):
-        o_ref[at] = total.astype(BF16)
+    out_units = make_units(plane, obuf, o_sent, o_landed, rows, OUT_UNITS, ("first",))
+
+    def finish(unit, total):
+        o_ref[unit.at] = total.astype(BF16)
 
     run_units(out_units, product_of(obuf, wo_ref, oacc, finish))
 
@@ -421,11 +447,13 @@
 
     @pl.when(pos < 2)
     def _():
-        to_across.wait_send()
+        for unit in range(IN_UNITS):
+            over(pos, unit, across).wait_send()
 
     @pl.when(pos >= 2)
     def _():
-        relay.wait_send()
+        for unit in range(IN_UNITS):
+            relay(across_slot, unit).wait_send()
 
     for d in order:
         @pl.when(seg + d < segments)
@@ -468,14 +496,14 @@
             pltpu.VMEM((HD, HD), BF16),
             pltpu.VMEM((HEADS, rows, HD), BF16),
             pltpu.VMEM((rows, out_columns), F32),
-            pltpu.SemaphoreType.REGULAR((3, 2)),
+            pltpu.SemaphoreType.REGULAR((segments - 1,)),
             dma((4,)),
             dma((IN_UNITS, 15)),
             dma((IN_UNITS, 15)),
             dma((6,)),
             dma((6,)),
-            dma((3,)),
-            dma((3,)),
+            dma((1 + 2 * IN_UNITS,)),
+            dma((1 + 2 * IN_UNITS,)),
             dma((3,)),
             dma((3,)),
             dma((segments - 1,)),

time: 72 us -> 70.2 us (0.975)
  the two profiles are of different devices: /device:TPU:16 before, /device:TPU:480 now
where the time goes in v4:
time: 70.2 us; the launch traced here: 69.6 us
  Pallas kernels  67.2 us (96%)
  local copies, waits for them, and re-layouts  1.67 us (2%)
    pallas_call x1, Pallas kernels, layer(): pl.pallas_call(functools.partial(layer_kernel, segments), out_shape=jax.S...  67.2 us
    unnamed x1, local copies, waits for them, and re-layouts  1.67 us

profile of v4, /device:TPU:480, one launch (start us, length us, event | category | flops | bytes accessed | tf_op | source)
XLA Modules:
  0.0 69.6 jit_solution(17597961312760257343)
XLA Ops:
  0.7 67.2 %layer.1 = bf16[512,256]{1,0:T(8,128)(2,1)} custom-call(f32[1]{0:T(128)S(6)} %copy.7.gate_ref, bf16[512,256]{1,0:T(8,128)(2,1)} %tokens_hbm.1, bf16[1,256]{1,0:T(2,128)(2,1)} %gain_hbm.1, bf16[16,256,384]{2,1,0:T(8,128)(2,1)} %bitcast.2, bf16[16,128,256]{2,1,0:T(8,128)(2,1)} %bitcast.3), custom_call_target="tpu_custom_call" | custom-call | tf_op jit(solution)/shard_map/layer/pallas_call | solution.py:470
  67.9 1.7 %copy.8 = bf16[512,256]{1,0:T(8,128)(2,1)} copy(bf16[512,256]{1,0:T(8,128)(2,1)} %layer.1) | data formatting | bytes 524288

commit v5 on v4

--- a/solution.py
+++ b/solution.py
@@ -341,23 +341,6 @@
             over(pos, unit, across).start()
 
     to_mate.start()
-    for copy in first:
-        copy.wait_recv()
-    here = pl.ds(pl.multiple_of(pos * piece, 16), piece)
-    total = term[pos].astype(F32)
-    for at in range(3):
-        total = total + parts[at].astype(F32)
-    outgoing[...] = total.astype(BF16)
-
-    def second(d):
-        return remote(outgoing, incoming.at[d - 1], b_sent.at[d - 1], b_landed.at[d - 1], later[d - 1])
-
-    order = sorted(range(1, segments), key=lambda d: -min(d, segments - d))
-    for d in order:
-        @pl.when(seg + d < segments)
-        def _():
-            pl.semaphore_wait(ready.at[d - 1], 1)
-            second(d).start()
 
     chunk = 128
 
@@ -387,6 +370,25 @@
             local_ref[at] = mixed
 
     attend(pos, True)
+
+    for copy in first:
+        copy.wait_recv()
+    here = pl.ds(pl.multiple_of(pos * piece, 16), piece)
+    total = term[pos].astype(F32)
+    for at in range(3):
+        total = total + parts[at].astype(F32)
+    outgoing[...] = total.astype(BF16)
+
+    def second(d):
+        return remote(outgoing, incoming.at[d - 1], b_sent.at[d - 1], b_landed.at[d - 1], later[d - 1])
+
+    order = sorted(range(1, segments), key=lambda d: -min(d, segments - d))
+    for d in order:
+        @pl.when(seg + d < segments)
+        def _():
+            pl.semaphore_wait(ready.at[d - 1], 1)
+            second(d).start()
+
     from_mate.wait_recv()
 
     @pl.when(mate_slot < pos)
@@ -398,13 +400,7 @@
         for unit in range(IN_UNITS):
             over(across_slot, unit, across).wait_recv()
             relay(across_slot, unit).start()
-        attend(across_slot, False)
-        for unit in range(IN_UNITS):
-            relay(relayed_slot, unit).wait_recv()
-        attend(relayed_slot, False)
-
-    gate = jax.nn.sigmoid(jnp.full((1, HD), gate_ref[0], F32))
-    local_ref[...] = local_ref[...] * ((1.0 - gate) / sum_ref[...])
+
     queries = feat(q_ref[...].astype(F32)).astype(BF16)
 
     share[...] = jnp.zeros_like(share)
@@ -413,21 +409,42 @@
         def _():
             second(d).wait_recv()
             share[...] += incoming[d - 1].astype(F32)
-    memory[here] = share[:piece].astype(BF16)
-    third = []
-    for step in (1, 2, 3):
-        copy = remote(memory.at[here], memory.at[here], c_sent.at[step - 1], c_landed.at[step - 1], peers[step])
-        copy.start()
-        third.append(copy)
+    def third(step):
+        return remote(memory.at[here], memory.at[here], c_sent.at[step - 1], c_landed.at[step - 1], peers[step])
+
+    @pl.when(seg == 0)
+    def _():
+        memory[...] = jnp.zeros_like(memory)
+
+    @pl.when(seg > 0)
+    def _():
+        memory[here] = share[:piece].astype(BF16)
+        for step in (2, 1, 3):
+            third(step).start()
+
+    @pl.when(pos >= 2)
+    def _():
+        attend(across_slot, False)
+        for unit in range(IN_UNITS):
+            relay(relayed_slot, unit).wait_recv()
+        attend(relayed_slot, False)
+
+    gate = jax.nn.sigmoid(jnp.full((1, HD), gate_ref[0], F32))
+    local_ref[...] = local_ref[...] * ((1.0 - gate) / sum_ref[...])
+
     pick = (lax.broadcasted_iota(jnp.int32, (8, HD), 0) == 0).astype(F32)
     norm = lax.dot_general(
         share[piece : piece + 8], pick, (((0,), (0,)), ((), ())), precision=HIGH, preferred_element_type=F32
     )
     denom = jnp.dot(queries, norm.astype(BF16), preferred_element_type=F32)
     weight = gate / jnp.maximum(denom, 1.0)
-    for step in (1, 2, 3):
-        there = memory.at[pl.ds(pl.multiple_of(lax.rem(pos + SPAN - step, SPAN) * piece, 16), piece)]
-        remote(there, there, c_sent.at[step - 1], c_landed.at[step - 1], peers[step]).wait_recv()
+
+    @pl.when(seg > 0)
+    def _():
+        for step in (1, 2, 3):
+            there = memory.at[pl.ds(pl.multiple_of(lax.rem(pos + SPAN - step, SPAN) * piece, 16), piece)]
+            remote(there, there, c_sent.at[step - 1], c_landed.at[step - 1], peers[step]).wait_recv()
+
     numer = jnp.dot(queries, memory[...], preferred_element_type=F32)
     obuf[h] = (numer * weight + local_ref[...]).astype(BF16)
 
@@ -442,8 +459,13 @@
     for unit in units + out_units:
         unit.finish()
     squares.finish()
-    for copy in [to_mate] + first + third:
+    for copy in [to_mate] + first:
         copy.wait_send()
+
+    @pl.when(seg > 0)
+    def _():
+        for step in (1, 2, 3):
+            third(step).wait_send()
 
     @pl.when(pos < 2)
     def _():

time: 70.2 us -> 69.7 us (level)
  no operation moved by 1% of the time
where the time goes in v5:
time: 69.7 us; the launch traced here: 69.6 us
  Pallas kernels  67.2 us (96%)
  local copies, waits for them, and re-layouts  1.67 us (2%)
    pallas_call x1, Pallas kernels, layer(): pl.pallas_call(functools.partial(layer_kernel, segments), out_shape=jax.S...  67.2 us
    unnamed x1, local copies, waits for them, and re-layouts  1.67 us

profile of v5, /device:TPU:480, one launch (start us, length us, event | category | flops | bytes accessed | tf_op | source)
XLA Modules:
  0.0 69.6 jit_solution(8836736248187999345)
XLA Ops:
  0.7 67.2 %layer.1 = bf16[512,256]{1,0:T(8,128)(2,1)} custom-call(f32[1]{0:T(128)S(6)} %copy.7.gate_ref, bf16[512,256]{1,0:T(8,128)(2,1)} %tokens_hbm.1, bf16[1,256]{1,0:T(2,128)(2,1)} %gain_hbm.1, bf16[16,256,384]{2,1,0:T(8,128)(2,1)} %bitcast.2, bf16[16,128,256]{2,1,0:T(8,128)(2,1)} %bitcast.3), custom_call_target="tpu_custom_call" | custom-call | tf_op jit(solution)/shard_map/layer/pallas_call | solution.py:492
  67.9 1.7 %copy.8 = bf16[512,256]{1,0:T(8,128)(2,1)} copy(bf16[512,256]{1,0:T(8,128)(2,1)} %layer.1) | data formatting | bytes 524288

commit v6 on v5

--- a/solution.py
+++ b/solution.py
@@ -337,7 +337,7 @@
 
     @pl.when(pos < 2)
     def _():
-        for unit in range(IN_UNITS):
+        for unit in range(IN_UNITS // 2):
             over(pos, unit, across).start()
 
     to_mate.start()
@@ -388,6 +388,11 @@
         def _():
             pl.semaphore_wait(ready.at[d - 1], 1)
             second(d).start()
+
+    @pl.when(pos < 2)
+    def _():
+        for unit in range(IN_UNITS // 2, IN_UNITS):
+            over(pos, unit, across).start()
 
     from_mate.wait_recv()
 

time: 69.7 us -> 67.6 us (0.970)
  Pallas kernels: 67.2 us -> 64.7 us
    pallas_call x1, Pallas kernels: 67.2 us -> 64.7 us  [layer(): pl.pallas_call(functools.partial(layer_kernel, segments), out_shape=jax.S...]
where the time goes in v6:
time: 67.6 us; the launch traced here: 67.1 us
  Pallas kernels  64.7 us (96%)
  local copies, waits for them, and re-layouts  1.67 us (2%)
    pallas_call x1, Pallas kernels, layer(): pl.pallas_call(functools.partial(layer_kernel, segments), out_shape=jax.S...  64.7 us
    unnamed x1, local copies, waits for them, and re-layouts  1.67 us

profile of v6, /device:TPU:480, one launch (start us, length us, event | category | flops | bytes accessed | tf_op | source)
XLA Modules:
  0.0 67.1 jit_solution(7705466548603911066)
XLA Ops:
  0.7 64.7 %layer.1 = bf16[512,256]{1,0:T(8,128)(2,1)} custom-call(f32[1]{0:T(128)S(6)} %copy.7.gate_ref, bf16[512,256]{1,0:T(8,128)(2,1)} %tokens_hbm.1, bf16[1,256]{1,0:T(2,128)(2,1)} %gain_hbm.1, bf16[16,256,384]{2,1,0:T(8,128)(2,1)} %bitcast.2, bf16[16,128,256]{2,1,0:T(8,128)(2,1)} %bitcast.3), custom_call_target="tpu_custom_call" | custom-call | tf_op jit(solution)/shard_map/layer/pallas_call | solution.py:497
  65.4 1.7 %copy.8 = bf16[512,256]{1,0:T(8,128)(2,1)} copy(bf16[512,256]{1,0:T(8,128)(2,1)} %layer.1) | data formatting | bytes 524288

commit v7 on v6

--- a/solution.py
+++ b/solution.py
@@ -328,12 +328,15 @@
     for at in range(SPAN):
         term[at, :piece] = whole[0][at * piece : (at + 1) * piece].astype(BF16)
         term[at, piece:] = jnp.broadcast_to(whole[1], (NORM_ROWS, HD)).astype(BF16)
-    first = []
-    for step in (2, 1, 3):
-        copy = remote(term.at[lax.rem(pos + step, SPAN)], parts.at[step - 1],
+
+    def first(step):
+        return remote(term.at[lax.rem(pos + step, SPAN)], parts.at[step - 1],
                       a_sent.at[step - 1], a_landed.at[step - 1], peers[step])
-        copy.start()
-        first.append(copy)
+
+    @pl.when(seg + 1 < segments)
+    def _():
+        for step in (2, 1, 3):
+            first(step).start()
 
     @pl.when(pos < 2)
     def _():
@@ -371,13 +374,15 @@
 
     attend(pos, True)
 
-    for copy in first:
-        copy.wait_recv()
     here = pl.ds(pl.multiple_of(pos * piece, 16), piece)
-    total = term[pos].astype(F32)
-    for at in range(3):
-        total = total + parts[at].astype(F32)
-    outgoing[...] = total.astype(BF16)
+
+    @pl.when(seg + 1 < segments)
+    def _():
+        total = term[pos].astype(F32)
+        for step in (1, 2, 3):
+            first(step).wait_recv()
+            total = total + parts[step - 1].astype(F32)
+        outgoing[...] = total.astype(BF16)
 
     def second(d):
         return remote(outgoing, incoming.at[d - 1], b_sent.at[d - 1], b_landed.at[d - 1], later[d - 1])
@@ -464,8 +469,12 @@
     for unit in units + out_units:
         unit.finish()
     squares.finish()
-    for copy in [to_mate] + first:
-        copy.wait_send()
+    to_mate.wait_send()
+
+    @pl.when(seg + 1 < segments)
+    def _():
+        for step in (1, 2, 3):
+            first(step).wait_send()
 
     @pl.when(seg > 0)
     def _():

time: 67.6 us -> 67.6 us (level)
  no operation moved by 1% of the time
where the time goes in v7:
time: 67.6 us; the launch traced here: 67 us
  Pallas kernels  64.7 us (96%)
  local copies, waits for them, and re-layouts  1.67 us (2%)
    pallas_call x1, Pallas kernels, layer(): pl.pallas_call(functools.partial(layer_kernel, segments), out_shape=jax.S...  64.7 us
    unnamed x1, local copies, waits for them, and re-layouts  1.67 us

profile of v7, /device:TPU:480, one launch (start us, length us, event | category | flops | bytes accessed | tf_op | source)
XLA Modules:
  0.0 67.0 jit_solution(5041316212515872746)
XLA Ops:
  0.7 64.7 %layer.1 = bf16[512,256]{1,0:T(8,128)(2,1)} custom-call(f32[1]{0:T(128)S(6)} %copy.7.gate_ref, bf16[512,256]{1,0:T(8,128)(2,1)} %tokens_hbm.1, bf16[1,256]{1,0:T(2,128)(2,1)} %gain_hbm.1, bf16[16,256,384]{2,1,0:T(8,128)(2,1)} %bitcast.2, bf16[16,128,256]{2,1,0:T(8,128)(2,1)} %bitcast.3), custom_call_target="tpu_custom_call" | custom-call | tf_op jit(solution)/shard_map/layer/pallas_call | solution.py:506
  65.4 1.7 %copy.8 = bf16[512,256]{1,0:T(8,128)(2,1)} copy(bf16[512,256]{1,0:T(8,128)(2,1)} %layer.1) | data formatting | bytes 524288
